TPU v7x, 512 devices: a whole 4x8x8 slice. The times are simulated.
512 devices in a mesh: vol: 128 (over x, z_hi, y, core), rep: 4 (over z_lo).
Axes of the slice: x: 4, y: 8, z: 8 (z_hi: 2, z_lo: 4; z = z_hi * 4 + z_lo), core: 2. Of those that a mesh axis runs over, the one named last changes fastest.
Arguments:
- displacement: float32 [3, 4, 512, 32, 128], P(None, None, 'vol', 'rep'), may hold values from -6 to 6
- body_force: float32 [3, 4, 512, 32, 128], P(None, None, 'vol', 'rep'), may hold values from -12 to 12
- stiffness: float32 [512, 32, 128], P('vol', 'rep'), may hold values from 0.5 to 4
- wet_cell: int32 [512, 128], P(('vol', 'rep')), may hold values from 0 to 4095, as said below
- wet_normal: float32 [3, 65536], P(None, ('vol', 'rep')), may hold values from -6 to 6
- route: int32 [65536, 1], P(('vol', 'rep')), may hold values from 0 to 127; in each aligned block of 128 rows (0 to 127, 128 to 255, ...) at most 2 rows name the same one
- tile_u: bfloat16 [16384, 32, 256], P(('vol', 'rep')), may hold values from -0.1875 to 0.1875
- tile_v: bfloat16 [16384, 32, 256], P(('vol', 'rep')), may hold values from -0.375 to 0.375
- tile_row: int32 [16384], P(('vol', 'rep')), may hold values from 0 to 3
- tile_col: int32 [16384], P(('vol', 'rep')), may hold values from 0 to 127
- tile_rank: int32 [16384], P(('vol', 'rep')), may hold values from 16 to 32
Outputs:
- updated: float32 [3, 4, 512, 32, 128], P(None, None, 'vol', 'rep')
- pressure: float32 [4, 131072], P(None, ('vol', 'rep'))
- wet_pressure: float32 [4, 65536], P(None, ('vol', 'rep'))
Inputs may be any that keep to these rules, and one draw needn't show every extreme that they name: `wet_cell`: the cells in a row are distinct. `route`: no partition routes more than 2 of its unknowns to one owner; some partition routes exactly 2.
All inputs are finite; a program needn't handle non-finite values.
Results may differ from a plain program's by a relative error of at most 0.015.
Values may be sent and summed in bfloat16 or wider, within the bound.
A program may use at most 64 MiB of HBM per device.

v0:
```python
import jax
import jax.numpy as jnp
from jax import lax
from jax.sharding import PartitionSpec as P

ITERS = 3


relax_factor = 0.8
mass_shift = 1.0


def with_halo(cells, sides, width):
    for axis, dim in sides:
        count = lax.axis_size(axis)
        ends = count - 1
        head = lax.slice_in_dim(cells, 0, width, axis=dim)
        tail = lax.slice_in_dim(cells, cells.shape[dim] - width, cells.shape[dim], axis=dim)
        cells = jnp.concatenate(
            [
                lax.ppermute(tail, axis, [(i, (i + 1) % count) for i in range(ends)]),
                cells,
                lax.ppermute(head, axis, [((i + 1) % count, i) for i in range(ends)]),
            ],
            axis=dim,
        )
    return cells


def slot_order(destination, owner_count):
    indicator = (destination[:, None] == jnp.arange(owner_count, dtype=jnp.int32)[None, :]).astype(
        jnp.int32
    )
    earlier = jnp.cumsum(indicator, axis=0) - indicator
    return jnp.sum(earlier * indicator, axis=1)


def shards(
    displacement,
    body_force,
    stiffness,
    wet_cell,
    wet_normal,
    route,
    tile_u,
    tile_v,
    tile_row,
    tile_col,
    tile_rank,
):
    n_vol = lax.axis_size("vol")
    n_rep = lax.axis_size("rep")
    components, incidences, span_x, span_y, span_z = displacement.shape
    slot_count = wet_cell.shape[1]
    cell_count = span_x * span_y * span_z
    capacity = max(2, 2 * slot_count // n_vol)
    region = n_vol * capacity
    tile_rows = tile_u.shape[2]
    per_region = region // tile_rows
    diagonal = mass_shift + 6.0 * stiffness
    coupling = stiffness / diagonal

    def neighbour_sum(volume):
        padded = with_halo(volume.astype(jnp.bfloat16), (("vol", 2), ("rep", 3)), 1).astype(
            volume.dtype
        )
        padded = jnp.pad(padded, ((0, 0), (0, 0), (0, 0), (0, 0), (1, 1)))
        summed = padded[:, :, 2:, 1:-1, 1:-1] + padded[:, :, :-2, 1:-1, 1:-1]
        summed = summed + padded[:, :, 1:-1, 2:, 1:-1] + padded[:, :, 1:-1, :-2, 1:-1]
        return summed + padded[:, :, 1:-1, 1:-1, 2:] + padded[:, :, 1:-1, 1:-1, :-2]

    def relax(volume, force):
        return volume + relax_factor * (
            force / diagonal - volume + coupling * neighbour_sum(volume)
        )

    volume = displacement
    for iteration in range(ITERS):
        volume = relax(volume, body_force)
    flattened = volume.reshape(components, incidences, cell_count)
    wet_cells = wet_cell[0]
    picked = jnp.take(flattened, wet_cells, axis=2)
    traces = jnp.sum(wet_normal[:, None, :] * picked, axis=0).astype(jnp.bfloat16)
    destination = route[:, 0]
    arrival = slot_order(destination, n_vol)
    position = destination * capacity + arrival
    placing = (position[:, None] == jnp.arange(region, dtype=jnp.int32)[None, :]).astype(
        jnp.bfloat16
    )
    packed = jnp.dot(traces, placing, preferred_element_type=jnp.float32).astype(jnp.bfloat16)
    packed = packed.reshape(incidences, n_vol, capacity)
    received = lax.all_to_all(packed, "vol", split_axis=1, concat_axis=1, tiled=True).reshape(
        incidences, region
    )
    surface = lax.all_gather(received, "vol", axis=1, tiled=True)
    x_blocks = surface.reshape(incidences, n_vol * per_region, tile_rows)
    chosen = jnp.take(x_blocks, tile_col, axis=1)
    coefficient = jnp.einsum("ktb,trb->tkr", chosen, tile_v, preferred_element_type=jnp.float32)
    retained = jnp.arange(tile_v.shape[1], dtype=jnp.int32)[None, :] < tile_rank[:, None]
    coefficient = jnp.where(retained[:, None, :], coefficient, 0.0).astype(jnp.bfloat16)
    contrib = jnp.einsum("tkr,trb->tkb", coefficient, tile_u, preferred_element_type=jnp.float32)
    row_select = (
        tile_row[:, None] == jnp.arange(n_rep * per_region, dtype=jnp.int32)[None, :]
    ).astype(jnp.float32)
    partial_rows = jnp.einsum("tkb,tn->knb", contrib, row_select, precision=lax.Precision.HIGHEST)
    partial_rows = partial_rows.reshape(incidences, n_rep * region)
    pressure = lax.psum_scatter(partial_rows, "rep", scatter_dimension=1, tiled=True)
    outgoing = pressure.astype(jnp.bfloat16).reshape(incidences, n_vol, capacity)
    returned = lax.all_to_all(outgoing, "vol", split_axis=1, concat_axis=1, tiled=True).reshape(
        incidences, region
    )
    wet_pressure = lax.dot_general(
        returned, placing, (((1,), (1,)), ((), ())), preferred_element_type=jnp.float32
    )
    load = jnp.zeros((components, incidences, cell_count), jnp.float32)
    load = load.at[:, :, wet_cells].set(-wet_normal[:, None, :] * wet_pressure[None, :, :])
    updated = relax(volume, body_force + load.reshape(displacement.shape))
    return (updated, pressure, wet_pressure)


def solution(mesh):
    return jax.shard_map(
        shards,
        mesh=mesh,
        in_specs=(
            P(None, None, "vol", "rep", None),
            P(None, None, "vol", "rep", None),
            P("vol", "rep", None),
            P(("vol", "rep"), None),
            P(None, ("vol", "rep")),
            P(("vol", "rep"), None),
            P(("vol", "rep"), None, None),
            P(("vol", "rep"), None, None),
            P(("vol", "rep")),
            P(("vol", "rep")),
            P(("vol", "rep")),
        ),
        out_specs=(
            P(None, None, "vol", "rep", None),
            P(None, ("vol", "rep")),
            P(None, ("vol", "rep")),
        ),
        check_vma=False,
    )
```

profile of v0, /device:TPU:1, one launch (start us, length us, event | category | flops | bytes accessed | tf_op | source)
XLA Modules:
  0.0 472.4 jit_solution(16405171624728426597)
XLA Ops:
  8.2 4.6 collective-permute-start
  12.8 5.5 %collective-permute-start.1 = (bf16[3,4,1,8,128]{4,3,2,1,0:T(8,128)(2,1)S(1)}, bf16[3,4,1,8,128]{4,3,2,1,0:T(8,128)(2,1)S(1)}, u32[]{:S(2)}, u32[]{:S(2)}) collective-permute-start(bf16[3,4,1,8,128]{4,3,2,1,0:T(8,128)(2,1)S(1)} %get-tuple-element.24), channel_id=1, source_target_pairs={{4,0},{8,4},{12,8},{16,12},{20,16},{24,20},{28,24},{32,28},{36,32}... | collective-permute-start | bytes 73736 | tf_op jit(solution)/shard_map/ppermute | solution.py:23
  22.3 1.3 collective-permute-start.2
  23.6 1.3 collective-permute-start.3
  25.5 3.1 collective-permute-done.3
  30.0 4.2 collective-permute-start.4
  34.2 1.9 collective-permute-start.5
  36.8 2.5 collective-permute-done.5
  39.5 4.0 collective-permute-start.6
  43.5 1.3 collective-permute-start.7
  45.4 3.0 collective-permute-done.7
  49.7 3.1 collective-permute-start.8
  52.8 1.9 collective-permute-start.9
  55.4 2.5 collective-permute-done.9
  58.0 3.6 collective-permute-start.10
  61.7 1.3 collective-permute-start.11
  63.8 2.6 collective-permute-done.11
  66.7 4.7 %copy.36 = f32[3,4,4,8,128]{1,0,4,3,2:T(4,128)} copy(f32[3,4,4,8,128]{4,3,2,1,0:T(8,128)S(1)} %get-tuple-element.4) | data formatting | bytes 393216 | tf_op jit(solution)/shard_map/add | solution.py:73
  71.5 4.1 gather_fusion
  77.0 33.3 %all-to-all-start = ((bf16[4,128,2]{0,2,1:T(2,128)(2,1)}), bf16[4,128,2]{0,2,1:T(2,128)(2,1)S(1)}, u32[]{:S(2)}, u32[]{:S(2)}) async-start(bf16[4,128,2]{0,2,1:T(2,128)(2,1)} %bitcast.9), calls=%async_computation | async-start | bytes 131072 | tf_op jit(solution)/shard_map/all_to_all | solution.py:92
  110.3 14.5 %all-to-all-done = bf16[4,128,2]{0,2,1:T(2,128)(2,1)S(1)} async-done(((bf16[4,128,2]{0,2,1:T(2,128)(2,1)}), bf16[4,128,2]{0,2,1:T(2,128)(2,1)S(1)}, u32[]{:S(2)}, u32[]{:S(2)}) %all-to-all-start) | async-done | bytes 2080 | tf_op jit(solution)/shard_map/all_to_all | solution.py:92
  124.8 252.8 %all_gather.3 = bf16[4,32768]{0,1:T(8,128)(2,1)} all-gather(bf16[4,256]{0,1:T(8,128)(2,1)S(1)} %bitcast.47), channel_id=1, replica_groups=mesh['vol'=128,'rep'=4] {'vol'}, dimensions={1}, use_global_device_ids=true | all-gather | bytes 264192 | tf_op jit(solution)/shard_map/all_gather | solution.py:95
  377.7 6.6 %copy.39 = bf16[4,128,256]{2,0,1:T(4,128)(2,1)S(1)} copy(bf16[4,128,256]{0,2,1:T(8,128)(2,1)} %bitcast.44) | data formatting | bytes 524288 | tf_op jit(solution)/shard_map/reshape | solution.py:96
  386.6 2.8 collective-permute-start.12
  389.5 1.9 collective-permute-start.13
  391.5 19.5 %reduce-scatter.4.cloned.1.call-done = f32[256,4]{1,0:T(8,128)} async-done(((f32[1024,4]{1,0:T(8,128)}), f32[256,4]{1,0:T(8,128)}) %reduce-scatter.4.cloned.1.call-update) | async-done | bytes 4112
  412.8 15.1 %all-to-all-start.1 = ((bf16[4,128,2]{0,2,1:T(2,128)(2,1)}), bf16[4,128,2]{0,2,1:T(2,128)(2,1)S(1)}, u32[]{:S(2)}, u32[]{:S(2)}) async-start(bf16[4,128,2]{0,2,1:T(2,128)(2,1)} %bitcast.14), calls=%async_computation.1 | async-start | bytes 131072 | tf_op jit(solution)/shard_map/all_to_all | solution.py:109
  428.1 2.8 collective-permute-start.14
  432.2 10.3 %all-to-all-done.1 = bf16[4,128,2]{0,2,1:T(2,128)(2,1)S(1)} async-done(((bf16[4,128,2]{0,2,1:T(2,128)(2,1)}), bf16[4,128,2]{0,2,1:T(2,128)(2,1)S(1)}, u32[]{:S(2)}, u32[]{:S(2)}) %all-to-all-start.1) | async-done | bytes 2080 | tf_op jit(solution)/shard_map/all_to_all | solution.py:109
  443.1 3.9 broadcast_in_dim.36
  447.0 12.6 %scatter_fusion = f32[3,4,4096]{1,0,2:T(4,128)} fusion(f32[3,4,4096]{1,0,2:T(4,128)} %broadcast_in_dim.36, s32[128]{0:T(128)S(1)} %fusion.47, f32[128,3,4]{2,1,0:T(4,128)S(1)} %multiply_bitcast_fusion), kind=kCustom, calls=%fused_computation.2 | custom fusion | bytes 18944 | tf_op jit(solution)/shard_map/scatter | solution.py:116
  459.6 4.9 %copy.43 = f32[3,4,4,8,128]{4,3,2,1,0:T(8,128)S(1)} copy(f32[3,4,4,8,128]{1,0,4,3,2:T(4,128)} %bitcast.43) | data formatting | bytes 393216 | tf_op jit(solution)/shard_map/reshape | solution.py:117
  (73 shorter events, 20.0 us)
Async XLA Ops:
  7.2 377.8 %copy-start = (bf16[32,32,256]{2,1,0:T(8,128)(2,1)S(1)}, bf16[32,32,256]{2,1,0:T(8,128)(2,1)}, u32[]{:S(2)}) copy-start(bf16[32,32,256]{2,1,0:T(8,128)(2,1)} %param.17) | copy-start | bytes 1572868
  7.2 59.4 %copy-start.1 = (f32[3,4,4,8,128]{4,3,2,1,0:T(8,128)S(1)}, f32[3,4,4,8,128]{4,3,2,1,0:T(8,128)}, u32[]{:S(2)}) copy-start(f32[3,4,4,8,128]{4,3,2,1,0:T(8,128)} %param.12) | copy-start | bytes 589828
  8.2 14.0 %collective-permute-start = (bf16[3,4,1,8,128]{4,3,2,1,0:T(8,128)(2,1)S(1)}, bf16[3,4,1,8,128]{4,3,2,1,0:T(8,128)(2,1)S(1)}, u32[]{:S(2)}, u32[]{:S(2)}) collective-permute-start(bf16[3,4,1,8,128]{4,3,2,1,0:T(8,128)(2,1)S(1)} %get-tuple-element.23), channel_id=1, source_target_pairs={{0,4},{4,8},{8,12},{12,16},{16,20},{20,24},{24,28},{28,32},{32,36}... | collective-permute-start | bytes 73736 | tf_op jit(solution)/shard_map/ppermute | solution.py:21
  12.8 9.4 %collective-permute-start.1 = (bf16[3,4,1,8,128]{4,3,2,1,0:T(8,128)(2,1)S(1)}, bf16[3,4,1,8,128]{4,3,2,1,0:T(8,128)(2,1)S(1)}, u32[]{:S(2)}, u32[]{:S(2)}) collective-permute-start(bf16[3,4,1,8,128]{4,3,2,1,0:T(8,128)(2,1)S(1)} %get-tuple-element.24), channel_id=1, source_target_pairs={{4,0},{8,4},{12,8},{16,12},{20,16},{24,20},{28,24},{32,28},{36,32}... | collective-permute-start | bytes 73736 | tf_op jit(solution)/shard_map/ppermute | solution.py:23
  22.3 3.3 collective-permute-start.2
  23.6 5.1 %collective-permute-start.3 = (bf16[3,4,6,1,128]{4,3,2,1,0:T(2,128)(2,1)S(1)}, bf16[3,4,6,1,128]{4,3,2,1,0:T(2,128)(2,1)S(1)}, u32[]{:S(2)}, u32[]{:S(2)}) collective-permute-start(bf16[3,4,6,1,128]{4,3,2,1,0:T(2,128)(2,1)S(1)} %get-tuple-element.16), channel_id=1, source_target_pairs={{1,0},{2,1},{3,2},{5,4},{6,5},{7,6},{9,8},{10,9},{11,10},{13,12},{... | collective-permute-start | bytes 55304 | tf_op jit(solution)/shard_map/ppermute | solution.py:23
  30.0 6.8 %collective-permute-start.4 = (bf16[3,4,1,8,128]{4,3,2,1,0:T(8,128)(2,1)S(1)}, bf16[3,4,1,8,128]{4,3,2,1,0:T(8,128)(2,1)S(1)}, u32[]{:S(2)}, u32[]{:S(2)}) collective-permute-start(bf16[3,4,1,8,128]{4,3,2,1,0:T(8,128)(2,1)S(1)} %get-tuple-element.21), channel_id=1, source_target_pairs={{0,4},{4,8},{8,12},{12,16},{16,20},{20,24},{24,28},{28,32},{32,36}... | collective-permute-start | bytes 73736 | tf_op jit(solution)/shard_map/ppermute | solution.py:21
  34.2 5.1 %collective-permute-start.5 = (bf16[3,4,1,8,128]{4,3,2,1,0:T(8,128)(2,1)S(1)}, bf16[3,4,1,8,128]{4,3,2,1,0:T(8,128)(2,1)S(1)}, u32[]{:S(2)}, u32[]{:S(2)}) collective-permute-start(bf16[3,4,1,8,128]{4,3,2,1,0:T(8,128)(2,1)S(1)} %get-tuple-element.22), channel_id=1, source_target_pairs={{4,0},{8,4},{12,8},{16,12},{20,16},{24,20},{28,24},{32,28},{36,32}... | collective-permute-start | bytes 73736 | tf_op jit(solution)/shard_map/ppermute | solution.py:23
  39.5 6.0 %collective-permute-start.6 = (bf16[3,4,6,1,128]{4,3,2,1,0:T(2,128)(2,1)S(1)}, bf16[3,4,6,1,128]{4,3,2,1,0:T(2,128)(2,1)S(1)}, u32[]{:S(2)}, u32[]{:S(2)}) collective-permute-start(bf16[3,4,6,1,128]{4,3,2,1,0:T(2,128)(2,1)S(1)} %get-tuple-element.13), channel_id=1, source_target_pairs={{0,1},{1,2},{2,3},{4,5},{5,6},{6,7},{8,9},{9,10},{10,11},{12,13},{... | collective-permute-start | bytes 55304 | tf_op jit(solution)/shard_map/ppermute | solution.py:21
  43.5 5.0 %collective-permute-start.7 = (bf16[3,4,6,1,128]{4,3,2,1,0:T(2,128)(2,1)S(1)}, bf16[3,4,6,1,128]{4,3,2,1,0:T(2,128)(2,1)S(1)}, u32[]{:S(2)}, u32[]{:S(2)}) collective-permute-start(bf16[3,4,6,1,128]{4,3,2,1,0:T(2,128)(2,1)S(1)} %get-tuple-element.14), channel_id=1, source_target_pairs={{1,0},{2,1},{3,2},{5,4},{6,5},{7,6},{9,8},{10,9},{11,10},{13,12},{... | collective-permute-start | bytes 55304 | tf_op jit(solution)/shard_map/ppermute | solution.py:23
  49.7 5.7 %collective-permute-start.8 = (bf16[3,4,1,8,128]{4,3,2,1,0:T(8,128)(2,1)S(1)}, bf16[3,4,1,8,128]{4,3,2,1,0:T(8,128)(2,1)S(1)}, u32[]{:S(2)}, u32[]{:S(2)}) collective-permute-start(bf16[3,4,1,8,128]{4,3,2,1,0:T(8,128)(2,1)S(1)} %get-tuple-element.19), channel_id=1, source_target_pairs={{0,4},{4,8},{8,12},{12,16},{16,20},{20,24},{24,28},{28,32},{32,36}... | collective-permute-start | bytes 73736 | tf_op jit(solution)/shard_map/ppermute | solution.py:21
  52.8 5.1 %collective-permute-start.9 = (bf16[3,4,1,8,128]{4,3,2,1,0:T(8,128)(2,1)S(1)}, bf16[3,4,1,8,128]{4,3,2,1,0:T(8,128)(2,1)S(1)}, u32[]{:S(2)}, u32[]{:S(2)}) collective-permute-start(bf16[3,4,1,8,128]{4,3,2,1,0:T(8,128)(2,1)S(1)} %get-tuple-element.20), channel_id=1, source_target_pairs={{4,0},{8,4},{12,8},{16,12},{20,16},{24,20},{28,24},{32,28},{36,32}... | collective-permute-start | bytes 73736 | tf_op jit(solution)/shard_map/ppermute | solution.py:23
  58.0 5.8 %collective-permute-start.10 = (bf16[3,4,6,1,128]{4,3,2,1,0:T(2,128)(2,1)S(1)}, bf16[3,4,6,1,128]{4,3,2,1,0:T(2,128)(2,1)S(1)}, u32[]{:S(2)}, u32[]{:S(2)}) collective-permute-start(bf16[3,4,6,1,128]{4,3,2,1,0:T(2,128)(2,1)S(1)} %get-tuple-element.11), channel_id=1, source_target_pairs={{0,1},{1,2},{2,3},{4,5},{5,6},{6,7},{8,9},{9,10},{10,11},{12,13},{... | collective-permute-start | bytes 55304 | tf_op jit(solution)/shard_map/ppermute | solution.py:21
  61.7 4.7 collective-permute-start.11
  77.0 47.9 %all-to-all-start = ((bf16[4,128,2]{0,2,1:T(2,128)(2,1)}), bf16[4,128,2]{0,2,1:T(2,128)(2,1)S(1)}, u32[]{:S(2)}, u32[]{:S(2)}) async-start(bf16[4,128,2]{0,2,1:T(2,128)(2,1)} %bitcast.9), calls=%async_computation | async-start | bytes 131072 | tf_op jit(solution)/shard_map/all_to_all | solution.py:92
  110.3 300.8 %reduce-scatter.4.cloned.1.call-start = ((), (), s32[]{:S(2)}) async-start(), calls=%async_computation.3 | async-start | bytes 655360
  124.8 260.1 %copy-start.2 = (bf16[32,32,256]{2,1,0:T(8,128)(2,1)S(1)}, bf16[32,32,256]{2,1,0:T(8,128)(2,1)}, u32[]{:S(2)}) copy-start(bf16[32,32,256]{2,1,0:T(8,128)(2,1)} %param.18) | copy-start | bytes 1572868
  124.8 260.5 %copy-start.6 = (s32[32]{0:T(128)S(1)}, s32[32]{0:T(128)}, u32[]{:S(2)}) copy-start(s32[32]{0:T(128)} %param.19) | copy-start | bytes 388
  124.8 266.6 %copy-start.4 = (f32[3,128]{1,0:T(4,128)S(1)}, f32[3,128]{1,0:T(4,128)}, u32[]{:S(2)}) copy-start(f32[3,128]{1,0:T(4,128)} %param.15) | copy-start | bytes 4612
  386.6 41.3 %collective-permute-start.12 = (bf16[3,4,1,8,128]{4,3,2,1,0:T(8,128)(2,1)S(1)}, bf16[3,4,1,8,128]{4,3,2,1,0:T(8,128)(2,1)S(1)}, u32[]{:S(2)}, u32[]{:S(2)}) collective-permute-start(bf16[3,4,1,8,128]{4,3,2,1,0:T(8,128)(2,1)S(1)} %get-tuple-element.17), channel_id=1, source_target_pairs={{0,4},{4,8},{8,12},{12,16},{16,20},{20,24},{24,28},{28,32},{32,36}... | collective-permute-start | bytes 73736 | tf_op jit(solution)/shard_map/ppermute | solution.py:21
  389.5 38.5 %collective-permute-start.13 = (bf16[3,4,1,8,128]{4,3,2,1,0:T(8,128)(2,1)S(1)}, bf16[3,4,1,8,128]{4,3,2,1,0:T(8,128)(2,1)S(1)}, u32[]{:S(2)}, u32[]{:S(2)}) collective-permute-start(bf16[3,4,1,8,128]{4,3,2,1,0:T(8,128)(2,1)S(1)} %get-tuple-element.18), channel_id=1, source_target_pairs={{4,0},{8,4},{12,8},{16,12},{20,16},{24,20},{28,24},{32,28},{36,32}... | collective-permute-start | bytes 73736 | tf_op jit(solution)/shard_map/ppermute | solution.py:23
  412.1 52.5 %copy-start.3 = (f32[4,256]{1,0:T(4,128)}, f32[4,256]{1,0:T(4,128)S(1)}, u32[]{:S(2)}) copy-start(f32[4,256]{1,0:T(4,128)S(1)} %copy.47) | copy-start | bytes 12292
  412.8 29.7 %all-to-all-start.1 = ((bf16[4,128,2]{0,2,1:T(2,128)(2,1)}), bf16[4,128,2]{0,2,1:T(2,128)(2,1)S(1)}, u32[]{:S(2)}, u32[]{:S(2)}) async-start(bf16[4,128,2]{0,2,1:T(2,128)(2,1)} %bitcast.14), calls=%async_computation.1 | async-start | bytes 131072 | tf_op jit(solution)/shard_map/all_to_all | solution.py:109
  428.1 36.5 %collective-permute-start.14 = (bf16[3,4,6,1,128]{4,3,2,1,0:T(2,128)(2,1)S(1)}, bf16[3,4,6,1,128]{4,3,2,1,0:T(2,128)(2,1)S(1)}, u32[]{:S(2)}, u32[]{:S(2)}) collective-permute-start(bf16[3,4,6,1,128]{4,3,2,1,0:T(2,128)(2,1)S(1)} %get-tuple-element.9), channel_id=1, source_target_pairs={{0,1},{1,2},{2,3},{4,5},{5,6},{6,7},{8,9},{9,10},{10,11},{12,13},{... | collective-permute-start | bytes 55304 | tf_op jit(solution)/shard_map/ppermute | solution.py:21
  430.9 33.6 %collective-permute-start.15 = (bf16[3,4,6,1,128]{4,3,2,1,0:T(2,128)(2,1)S(1)}, bf16[3,4,6,1,128]{4,3,2,1,0:T(2,128)(2,1)S(1)}, u32[]{:S(2)}, u32[]{:S(2)}) collective-permute-start(bf16[3,4,6,1,128]{4,3,2,1,0:T(2,128)(2,1)S(1)} %get-tuple-element.10), channel_id=1, source_target_pairs={{1,0},{2,1},{3,2},{5,4},{6,5},{7,6},{9,8},{10,9},{11,10},{13,12},{... | collective-permute-start | bytes 55304 | tf_op jit(solution)/shard_map/ppermute | solution.py:23
  442.7 21.8 %copy-start.5 = (f32[4,128]{1,0:T(4,128)}, f32[4,128]{1,0:T(4,128)S(1)}, u32[]{:S(2)}) copy-start(f32[4,128]{1,0:T(4,128)S(1)} %fusion.28) | copy-start | bytes 6148
Sparse Core Ops, SparseCore 0:
  386.7 24.2 reduce-scatter.3
where the time goes:
time: 474 us; the launch traced here: 472 us
  blocking collectives  253 us (53%)
  starting transfers between devices  91.4 us (19%)
  waiting for transfers between devices  58.2 us (12%)
  local copies, waits for them, and re-layouts  42.2 us (9%)
  between operations  14.4 us (3%)
  other arithmetic  12.4 us (3%)
    all_gather x1, blocking collectives, shards(): surface = lax.all_gather(received, 'vol', axis=1, tiled=True)  253 us
    all_to_all x1, starting transfers between devices, shards(): lax.all_to_all(packed, 'vol', split_axis=1, concat_axis=1, tiled=True)  33.3 us
    ppermute x8, starting transfers between devices, with_halo(): lax.ppermute(tail, axis, [(i, (i + 1) % count) for i in range(ends)])  26.5 us
    unnamed x2, waiting for transfers between devices  19.6 us
    ppermute x8, starting transfers between devices, with_halo(): lax.ppermute(head, axis, [((i + 1) % count, i) for i in range(ends)])  16.4 us
    all_to_all x1, starting transfers between devices, shards(): lax.all_to_all(outgoing, 'vol', split_axis=1, concat_axis=1, tiled=True)  15.1 us
    all_to_all x1, waiting for transfers between devices, shards(): lax.all_to_all(packed, 'vol', split_axis=1, concat_axis=1, tiled=True)  14.5 us
    ppermute x8, waiting for transfers between devices, with_halo(): lax.ppermute(head, axis, [((i + 1) % count, i) for i in range(ends)])  13.8 us
  transfers between devices with their start and end apart: 19, of which 8 were waited for; matrix products, arithmetic and copies ran while one was open for 7% of the time, Pallas kernels for 0%

commit v1 on v0

v1 whole, which is shorter than its diff:
```python
import jax
import jax.numpy as jnp
from jax import lax
from jax.experimental import pallas as pl
from jax.experimental.pallas import tpu as pltpu
from jax.sharding import PartitionSpec as P

MESH = pl.DeviceIdType.MESH
relax_factor = 0.8
mass_shift = 1.0

F32 = jnp.float32
BF16 = jnp.bfloat16
I32 = jnp.int32

NX, NZH, NY, NC = 4, 2, 8, 2
NR = 4
NHI = NX * NZH
NLO = NY * NC
NV = NHI * NLO
SLOTS = 128
COMP = 12
TILES, RANK = 32, 32
TQ = TILES * RANK

NT = (((1,), (1,)), ((), ()))


def dot(a, b):
    return jnp.dot(a, b, preferred_element_type=F32)


def dot_nt(a, b):
    return lax.dot_general(a, b, NT, preferred_element_type=F32)


def iota(shape, dim):
    return lax.broadcasted_iota(I32, shape, dim)


def onehot(condition, dtype=BF16):
    return jnp.where(condition, 1.0, 0.0).astype(F32).astype(dtype)


def pairs(tiles):
    lead = 1
    for size in tiles.shape[:-2]:
        lead *= size
    return tiles.reshape(lead // 2, 16, 128).astype(BF16)


def unpairs(tiles, lead):
    return tiles.astype(F32).reshape(*lead, 8, 128)


def neighbours(inner, low, high):
    rows = inner.shape[1]
    lane = iota(inner.shape, 2)
    total = low + high
    total = total + pltpu.roll(inner, 1, 1) + pltpu.roll(inner, rows - 1, 1)
    total = total + jnp.where(lane == 0, 0.0, pltpu.roll(inner, 1, 2))
    return total + jnp.where(lane == 127, 0.0, pltpu.roll(inner, 127, 2))


def body(
    disp, force, stiff, wcell, wnorm, route, tu_any, tv_any, trow, tcol, trank,
    out_u, out_p, out_w,
    tu, tv, vol_s, vol_r, rep_s, rep_r, cor_s, cor_r, fvol_s, fvol_r, frep_s, frep_r,
    w_ext, f_ext, c_ext, field, base, scale,
    vdt, ud, ol, rowhot, armask, place, sel_t, diag_m, row_m, sel_lo, lo_hot, ha_hot,
    ra, g, zs, zr, xb, ws, wr,
    load_sem, halo_ss, halo_rs, fhalo_ss, fhalo_rs, ph_ss, ph_rs,
):
    v = lax.axis_index("vol")
    r = lax.axis_index("rep")
    hi, lo = v // NLO, lax.rem(v, NLO)
    x, zh = hi // NZH, lax.rem(hi, NZH)
    y, c = lo // NC, lax.rem(lo, NC)

    def vol_of(x_, zh_, y_, c_):
        return ((x_ * NZH + zh_) * NY + y_) * NC + c_

    hi_peers = [(lax.rem(hi + j, NHI) * NLO + lo, r) for j in range(1, NHI)]
    y_peers = [(vol_of(x, zh, lax.rem(y + j, NY), c), r) for j in range(1, NY)]
    core_peer = (vol_of(x, zh, y, 1 - c), r)
    lo_at = [lax.rem(lo + j, NLO) for j in range(1, NLO)]
    lo_peers = [(hi * NLO + at, r) for at in lo_at]
    x_peers = [(vol_of(lax.rem(x + j, NX), zh, y, c), r) for j in range(1, NX)]
    z_at = [(zh, lax.rem(r + j, NR)) for j in range(1, NR)] + [(1 - zh, lax.rem(r + j, NR)) for j in range(NR)]
    z_peers = [(vol_of(x, zh_, y, c), r_) for zh_, r_ in z_at]
    up_v, down_v = lax.rem(v + 1, NV), lax.rem(v + NV - 1, NV)
    up_r, down_r = lax.rem(r + 1, NR), lax.rem(r + NR - 1, NR)
    halo_peers = [(up_v, r), (down_v, r)] + [(a, b) for a in (up_v, down_v) for b in (up_r, down_r)]

    barrier = pltpu.get_barrier_semaphore()
    greeted = hi_peers + lo_peers + z_peers + halo_peers
    for peer in greeted:
        pl.semaphore_signal(barrier, inc=1, device_id=peer, device_id_type=MESH)

    load_u = pltpu.make_async_copy(tu_any, tu, load_sem.at[0])
    load_v = pltpu.make_async_copy(tv_any, tv, load_sem.at[1])
    load_u.start()
    load_v.start()

    row3 = iota((COMP, 4, 8, 128), 2)
    row_c = iota((COMP, 8, 128), 1)
    for side in (0, 1):
        first = 1 - side
        vol_s[side, 0:18] = pairs(disp[:, first:first + 3])
        vol_s[side, 18:30] = pairs(force[:, 2 - 2 * side:4 - 2 * side])
        vol_s[side, 30:31] = pairs(stiff[2 - 2 * side:4 - 2 * side])
    force_up = pltpu.roll(force[...].reshape(COMP * 4, 8, 128), 4, 1).reshape(COMP, 4, 8, 128)
    rep_s[0, 0:24] = pairs(jnp.where(row3 >= 5, disp[...], force_up))
    rep_s[1, 0:24] = pairs(jnp.where(row3 <= 2, disp[...], force_up))
    for side in (0, 1):
        rep_s[side, 24:26] = pairs(stiff[...])
        edge, second = (3, 2) if side == 0 else (0, 1)
        w_e, w_2, f_e = disp[:, edge], disp[:, second], force[:, edge]
        s_e = jnp.broadcast_to(stiff[edge:edge + 1], (COMP, 8, 128))
        w_2 = pltpu.roll(w_2, 4, 1)
        up = jnp.where(row_c >= 6, w_e, jnp.where(row_c == 3, w_2, jnp.where(row_c == 1, pltpu.roll(f_e, 2, 1), pltpu.roll(s_e, 1, 1))))
        down = jnp.where(row_c <= 1, w_e, jnp.where(row_c == 4, w_2, jnp.where(row_c == 6, pltpu.roll(f_e, 6, 1), pltpu.roll(s_e, 7, 1))))
        cor_s[side, 0] = pairs(up)
        cor_s[side, 1] = pairs(down)

    vol_to = [v < NV - 1, v > 0]
    vol_from = [v > 0, v < NV - 1]
    rep_to = [r < NR - 1, r > 0]
    rep_from = [r > 0, r < NR - 1]
    vol_dev, rep_dev = [up_v, down_v], [up_r, down_r]

    moves = []
    for s in (0, 1):
        moves.append((vol_s.at[s], vol_r.at[s], s, (vol_dev[s], r), vol_to[s], vol_from[s]))
    for s in (0, 1):
        for t in (0, 1):
            moves.append((cor_s.at[s, t], cor_r.at[s, t], 4 + 2 * s + t, (vol_dev[s], rep_dev[t]),
                          jnp.logical_and(vol_to[s], rep_to[t]), jnp.logical_and(vol_from[s], rep_from[t])))
    for t in (0, 1):
        moves.append((rep_s.at[t], rep_r.at[t], 2 + t, (v, rep_dev[t]), rep_to[t], rep_from[t]))

    def remote(src, dst, ss, rs, dev):
        return pltpu.make_async_remote_copy(src_ref=src, dst_ref=dst, send_sem=ss, recv_sem=rs, device_id=dev, device_id_type=MESH)

    for src, dst, at, dev, sends, comes in moves:
        @pl.when(jnp.logical_not(comes))
        def _():
            dst[...] = jnp.zeros(dst.shape, BF16)

    pl.semaphore_wait(barrier, len(greeted))

    for src, dst, at, dev, sends, comes in moves:
        @pl.when(sends)
        def _():
            remote(src, dst, halo_ss.at[at], halo_rs.at[at], dev).start()

    route_row = route[...]
    route_sq = jnp.broadcast_to(route_row, (SLOTS, SLOTS))
    route_col = jnp.transpose(route_sq.astype(F32)).astype(I32)
    sub = iota((SLOTS, SLOTS), 0)
    lane = iota((SLOTS, SLOTS), 1)
    earlier = jnp.where(jnp.logical_and(route_col == route_sq, sub < lane), 1.0, 0.0)
    arrival = jnp.sum(earlier, axis=0, keepdims=True).astype(I32)
    place[...] = onehot(sub == route_sq)
    armask[...] = jnp.where(iota((8, SLOTS), 0) // 4 == jnp.broadcast_to(arrival, (8, SLOTS)), 1.0, 0.0)
    cell = wcell[...]
    z_one = onehot(sub == jnp.broadcast_to(lax.rem(cell, 128), (SLOTS, SLOTS)))
    ol[0:128] = z_one
    ol[128:256] = z_one
    rowhot[...] = jnp.where(iota((32, SLOTS), 0) == jnp.broadcast_to(cell // 128, (32, SLOTS)), 1.0, 0.0)
    lo_t = jnp.where(sub == jnp.broadcast_to(lax.rem(route_row, NLO), (SLOTS, SLOTS)), 1.0, 0.0)
    lo_hot[...] = jnp.transpose(lo_t).astype(BF16)
    ha = route_row // NLO * 2 + arrival
    ha_t = jnp.where(sub // 4 == jnp.broadcast_to(ha, (SLOTS, SLOTS)), 1.0, 0.0)
    ha_hot[...] = jnp.transpose(ha_t)
    sel_lo[...] = onehot(iota((NLO, NV), 1) == iota((NLO, NV), 0) + hi * NLO)

    spread = onehot(iota((TILES, TQ), 1) // RANK == iota((TILES, TQ), 0))
    lists = jnp.concatenate([jnp.broadcast_to(trank[...], (4, TILES)), jnp.broadcast_to(trow[...], (4, TILES))], axis=0)
    over = dot(lists.astype(F32).astype(BF16), spread)
    rank_l, row_l = over[0:1], over[4:5]
    lane_q = lax.rem(iota((TILES, TQ), 1), RANK).astype(F32)
    diag_m[...] = jnp.where(lane_q < jnp.broadcast_to(rank_l, (TILES, TQ)), spread.astype(F32), 0.0)
    row_m[...] = jnp.where(iota((32, TQ), 0) // 8 == jnp.broadcast_to(row_l, (32, TQ)).astype(I32), 1.0, 0.0)
    col_t = jnp.where(iota((128, TILES), 0) == jnp.broadcast_to(tcol[...], (128, TILES)), 1.0, 0.0)
    col_t = jnp.concatenate([col_t, jnp.zeros((128, 96), F32)], axis=1)
    sel_t[...] = jnp.transpose(col_t)[0:TILES].astype(BF16)

    load_v.wait()
    load_u.wait()
    at_b, at_g = iota((256, 256), 0), iota((256, 256), 1)
    source = lax.rem(at_b // 2, 8) * 32 + lax.rem(at_b // 16, 8) * 4 + at_b // 128 * 2 + lax.rem(at_b, 2)
    perm_v = onehot(at_g == source)
    vdt[...] = dot_nt(perm_v, tv[...].reshape(TQ, 256)).astype(BF16)
    split = at_b == lax.rem(at_g, 128) * 2 + at_g // 128
    ud[...] = dot(tu[...].reshape(TQ, 256), onehot(split)).astype(BF16)

    w_ext[:, 3:7, 0:8] = disp[...]
    w_ext[:, 0:1, 8:16] = jnp.zeros((COMP, 1, 8, 128), F32)
    w_ext[:, 9:10, 8:16] = jnp.zeros((COMP, 1, 8, 128), F32)
    s_own = stiff[...]
    own_inv = relax_factor / (mass_shift + 6.0 * s_own)
    scale[...] = own_inv
    c_ext[2:6, 0:8] = own_inv * s_own
    f_ext[:, 2:6, 0:8] = force[...] * own_inv[None]

    for src, dst, at, dev, sends, comes in moves:
        @pl.when(comes)
        def _():
            remote(src, dst, halo_ss.at[at], halo_rs.at[at], dev).wait_recv()

    for s in (0, 1):
        w_ext[:, 7 * s:7 * s + 3, 0:8] = unpairs(vol_r[s, 0:18], (COMP, 3))
        s_v = unpairs(vol_r[s, 30:31], (2,))
        inv = relax_factor / (mass_shift + 6.0 * s_v)
        c_ext[6 * s:6 * s + 2, 0:8] = inv * s_v
        f_ext[:, 6 * s:6 * s + 2, 0:8] = unpairs(vol_r[s, 18:30], (COMP, 2)) * inv[None]
    low_r, high_r = unpairs(rep_r[0, 0:24], (COMP, 4)), unpairs(rep_r[1, 0:24], (COMP, 4))
    w_ext[:, 3:7, 8:16] = jnp.where(row3 <= 2, high_r, low_r)
    s_b = jnp.where(iota((4, 8, 128), 1) <= 3, unpairs(rep_r[1, 24:26], (4,)), unpairs(rep_r[0, 24:26], (4,)))
    inv = relax_factor / (mass_shift + 6.0 * s_b)
    c_ext[2:6, 8:16] = inv * s_b
    f_b = pltpu.roll(jnp.where(row3 >= 4, high_r, low_r).reshape(COMP * 4, 8, 128), 4, 1).reshape(COMP, 4, 8, 128)
    f_ext[:, 2:6, 8:16] = f_b * inv[None]
    zero_plane = jnp.zeros((1, 8, 128), F32)
    for s in (0, 1):
        low_c, high_c = unpairs(cor_r[s, 0], (COMP,)), unpairs(cor_r[s, 1], (COMP,))
        near, far = (2, 1) if s == 0 else (7, 8)
        w_ext[:, near, 8:16] = jnp.where(row_c <= 3, high_c, low_c)
        w_ext[:, far, 8:16] = jnp.where(row_c <= 3, pltpu.roll(high_c, 4, 1), pltpu.roll(low_c, 4, 1))
        s_c = jnp.where(row_c[0] <= 3, pltpu.roll(high_c[0], 1, 0), pltpu.roll(low_c[0], 7, 0))
        s_c = jnp.where(jnp.logical_or(row_c[0] == 0, row_c[0] == 7), s_c, 0.0)
        f_c = jnp.where(row_c <= 3, pltpu.roll(high_c, 2, 1), pltpu.roll(low_c, 6, 1))
        inv = relax_factor / (mass_shift + 6.0 * s_c)
        c_near, c_far = (1, 0) if s == 0 else (6, 7)
        c_ext[c_near, 8:16] = inv * s_c
        f_ext[:, c_near, 8:16] = f_c * inv[None]
        c_ext[c_far:c_far + 1, 8:16] = zero_plane
        f_ext[:, c_far, 8:16] = jnp.zeros((COMP, 8, 128), F32)

    keep = 1.0 - relax_factor

    def sweeps(i, carry):
        w = w_ext[i]
        f, cc = f_ext[i], c_ext[...]
        w = keep * w[1:9] + f + cc * neighbours(w[1:9], w[0:8], w[2:10])
        w = keep * w[1:7] + f[1:7] + cc[1:7] * neighbours(w[1:7], w[0:6], w[2:8])
        w = keep * w[1:5] + f[2:6] + cc[2:6] * neighbours(w[1:5], w[0:4], w[2:6])
        field[i] = w[:, 0:8]
        return carry

    lax.fori_loop(0, COMP, sweeps, 0)

    flat = field[...].reshape(COMP * 32, 128)
    upper = flat.astype(BF16)
    lower = (flat - upper.astype(F32)).astype(BF16)
    picked = dot(jnp.concatenate([upper, lower], axis=1), ol[...]).reshape(COMP, 32, SLOTS)
    normal = wnorm[...]
    picked = jnp.sum(picked * rowhot[...][None], axis=1)
    traces = normal[0:1] * picked[0:4] + normal[1:2] * picked[4:8] + normal[2:3] * picked[8:12]
    traces = jnp.concatenate([traces, traces], axis=0) * armask[...]
    message = dot_nt(traces.astype(BF16), place[...])

    ra[hi] = message
    for peer in hi_peers:
        remote(ra.at[hi], ra.at[hi], ph_ss.at[0], ph_rs.at[0], peer).start()

    row_f = iota((COMP, 8, 128), 1)
    fvol_s[0] = pairs(field[:, 3])
    fvol_s[1] = pairs(field[:, 0])
    for t in (0, 1):
        acc = jnp.zeros((COMP, 8, 128), F32)
        for p in range(4):
            shift = p + 1 if t == 0 else p
            rolled = field[:, p] if shift == 0 else pltpu.roll(field[:, p], shift, 1)
            acc = jnp.where(row_f == p, rolled, acc)
        frep_s[t] = pairs(acc)
    fmoves = []
    for s in (0, 1):
        fmoves.append((fvol_s.at[s], fvol_r.at[s], s, (vol_dev[s], r), vol_to[s], vol_from[s]))
        fmoves.append((frep_s.at[s], frep_r.at[s], 2 + s, (v, rep_dev[s]), rep_to[s], rep_from[s]))
    for src, dst, at, dev, sends, comes in fmoves:
        @pl.when(sends)
        def _():
            remote(src, dst, fhalo_ss.at[at], fhalo_rs.at[at], dev).start()

        @pl.when(jnp.logical_not(comes))
        def _():
            dst[...] = jnp.zeros(dst.shape, BF16)

    to_row, from_row = iota((64, 64), 0), iota((64, 64), 1)
    wanted = lax.rem(to_row, 16) // 2 * 8 + lax.rem(to_row, 2) * 4 + to_row // 16
    reorder = onehot(from_row == wanted)

    def wait_all(region, at, peer):
        remote(region, region, ph_ss.at[at], ph_rs.at[at], peer).wait_recv()

    wait_all(ra.at[pl.ds(0, NHI - 1)], 0, hi_peers[0])
    mine = dot(reorder, ra[...].reshape(64, 128).astype(BF16)).astype(BF16).reshape(4, 16, 128)
    g[c, y] = mine
    for peer in y_peers:
        remote(g.at[c, y], g.at[c, y], ph_ss.at[1], ph_rs.at[1], peer).start()
    wait_all(g.at[c, pl.ds(0, NY - 1)], 1, y_peers[0])
    remote(g.at[c], g.at[c], ph_ss.at[2], ph_rs.at[2], core_peer).start()

    for src, dst, at, dev, sends, comes in fmoves:
        @pl.when(comes)
        def _():
            remote(src, dst, fhalo_ss.at[at], fhalo_rs.at[at], dev).wait_recv()

    wait_all(g.at[c], 2, core_peer)

    pick = sel_t[...]
    chosen = jnp.concatenate([dot_nt(pick, g[:, :, k].reshape(256, 128)) for k in range(4)], axis=0).astype(BF16)
    every = dot(chosen, vdt[...])
    coef = jnp.sum(every.reshape(4, TILES, TQ) * diag_m[...][None], axis=1)
    coef = jnp.concatenate([coef, coef], axis=0)
    spread_c = (jnp.concatenate([coef] * 4, axis=0) * row_m[...]).astype(BF16)
    parts = dot(spread_c, ud[...])
    take = lax.rem(iota((32, 128), 0), 8) < 4
    parts = jnp.where(take, parts[:, 0:128], parts[:, 128:256])
    zs[...] = parts.reshape(4, 8, 128)

    mine_at = zh * NR + r
    for (zh_, r_), peer in zip(z_at, z_peers):
        remote(zs.at[r_], zr.at[mine_at], ph_ss.at[3], ph_rs.at[3], peer).start()
    zr[mine_at] = zs[r]

    low_f, high_f = unpairs(fvol_r[0], (COMP,)), unpairs(fvol_r[1], (COMP,))
    low_y, high_y = unpairs(frep_r[0], (COMP,)), unpairs(frep_r[1], (COMP,))
    for p in range(4):
        w = field[:, p]
        total = (field[:, p - 1] if p > 0 else low_f) + (field[:, p + 1] if p < 3 else high_f)
        before = pltpu.roll(low_y, 8 - p, 1) if p > 0 else low_y
        after = pltpu.roll(high_y, 7 - p, 1)
        total = total + jnp.where(row_f == 0, before, pltpu.roll(w, 1, 1))
        total = total + jnp.where(row_f == 7, after, pltpu.roll(w, 7, 1))
        lane_f = iota((COMP, 8, 128), 2)
        total = total + jnp.where(lane_f == 0, 0.0, pltpu.roll(w, 1, 2))
        total = total + jnp.where(lane_f == 127, 0.0, pltpu.roll(w, 127, 2))
        base[:, p] = keep * w + f_ext[:, 2 + p, 0:8] + c_ext[2 + p, 0:8][None] * total

    wait_all(zr.at[pl.ds(0, 2 * NR - 1)], 3, z_peers[0])
    sums = jnp.sum(zr[...].reshape(NZH, NR, 8, 128), axis=1)
    xb[x] = sums.reshape(16, 128).astype(BF16)
    for peer in x_peers:
        remote(xb.at[x], xb.at[x], ph_ss.at[4], ph_rs.at[4], peer).start()
    own = jnp.where(zh == 0, sums[0], sums[1])
    wide = jnp.concatenate([own[0:4], own[4:8]], axis=1)
    join = jnp.where(at_g == lax.rem(at_b, 128) * 2 + at_b // 128, 1.0, 0.0)
    out_p[...] = jnp.dot(wide, join, precision=lax.Precision.HIGHEST, preferred_element_type=F32)

    wait_all(xb.at[pl.ds(0, NX - 1)], 4, x_peers[0])
    gathered = xb[...].reshape(64, 128)
    gathered = jnp.concatenate([gathered, jnp.zeros((64, 128), BF16)], axis=0)
    ws[...] = dot_nt(sel_lo[...], gathered).reshape(NLO, 1, 128)
    for at, peer in zip(lo_at, lo_peers):
        remote(ws.at[at], wr.at[lo], ph_ss.at[5], ph_rs.at[5], peer).start()
    wr[lo] = ws[lo]
    wait_all(wr.at[pl.ds(0, NLO - 1)], 5, lo_peers[0])

    got = wr[...].reshape(NLO, 128).astype(BF16)
    got = jnp.concatenate([got, jnp.zeros((128 - NLO, 128), BF16)], axis=0)
    per_slot = (dot(lo_hot[...], got) * ha_hot[...]).astype(BF16)
    wave = onehot(lax.rem(iota((8, 128), 1), 4) == iota((8, 128), 0))
    wet = dot_nt(wave, per_slot)[0:4]
    out_w[...] = wet

    normal = -wnorm[...]
    load = jnp.concatenate([normal[i:i + 1] * wet for i in range(3)], axis=0)
    rows = (load[:, None, :] * rowhot[...][None]).reshape(COMP * 32, SLOTS)
    upper = rows.astype(BF16)
    lower = (rows - upper.astype(F32)).astype(BF16)
    z_one = ol[0:128]
    placed = dot_nt(jnp.concatenate([upper, lower], axis=1), jnp.concatenate([z_one, z_one], axis=1))
    out_u[...] = base[...] + scale[...][None] * placed.reshape(COMP, 4, 8, 128)

    for src, dst, at, dev, sends, comes in moves:
        @pl.when(sends)
        def _():
            remote(src, dst, halo_ss.at[at], halo_rs.at[at], dev).wait_send()
    for src, dst, at, dev, sends, comes in fmoves:
        @pl.when(sends)
        def _():
            remote(src, dst, fhalo_ss.at[at], fhalo_rs.at[at], dev).wait_send()

    def sent(region, at, peer):
        remote(region, region, ph_ss.at[at], ph_rs.at[at], peer).wait_send()

    sent(ra.at[pl.ds(0, NHI - 1)], 0, hi_peers[0])
    sent(g.at[c, pl.ds(0, NY - 1)], 1, y_peers[0])
    sent(g.at[c], 2, core_peer)
    sent(zr.at[pl.ds(0, 2 * NR - 1)], 3, z_peers[0])
    sent(xb.at[pl.ds(0, NX - 1)], 4, x_peers[0])
    sent(wr.at[pl.ds(0, NLO - 1)], 5, lo_peers[0])


def shards(displacement, body_force, stiffness, wet_cell, wet_normal, route, tile_u, tile_v, tile_row, tile_col, tile_rank):
    vmem = pl.BlockSpec(memory_space=pltpu.VMEM)
    anywhere = pl.BlockSpec(memory_space=pl.ANY)
    V = pltpu.VMEM
    updated, pressure, wet = pl.pallas_call(
        body,
        out_shape=(
            jax.ShapeDtypeStruct((COMP, 4, 8, 128), F32),
            jax.ShapeDtypeStruct((4, 256), F32),
            jax.ShapeDtypeStruct((4, SLOTS), F32),
        ),
        in_specs=[vmem] * 6 + [anywhere] * 2 + [vmem] * 3,
        out_specs=(vmem, vmem, vmem),
        scratch_shapes=[
            V((TILES, RANK, 256), BF16), V((TILES, RANK, 256), BF16),
            V((2, 31, 16, 128), BF16), V((2, 31, 16, 128), BF16),
            V((2, 26, 16, 128), BF16), V((2, 26, 16, 128), BF16),
            V((2, 2, 6, 16, 128), BF16), V((2, 2, 6, 16, 128), BF16),
            V((2, 6, 16, 128), BF16), V((2, 6, 16, 128), BF16),
            V((2, 6, 16, 128), BF16), V((2, 6, 16, 128), BF16),
            V((COMP, 10, 16, 128), F32), V((COMP, 8, 16, 128), F32), V((8, 16, 128), F32),
            V((COMP, 4, 8, 128), F32), V((COMP, 4, 8, 128), F32), V((4, 8, 128), F32),
            V((256, TQ), BF16), V((TQ, 256), BF16), V((256, SLOTS), BF16), V((32, SLOTS), F32),
            V((8, SLOTS), F32), V((128, SLOTS), BF16), V((TILES, 128), BF16), V((TILES, TQ), F32),
            V((32, TQ), F32), V((NLO, NV), BF16), V((SLOTS, 128), BF16), V((SLOTS, 128), F32),
            V((NHI, 8, 128), F32), V((NC, NY, 4, 16, 128), BF16),
            V((NR, 8, 128), F32), V((NZH * NR, 8, 128), F32), V((NX, 16, 128), BF16),
            V((NLO, 1, 128), F32), V((NLO, 1, 128), F32),
            pltpu.SemaphoreType.DMA((2,)),
            pltpu.SemaphoreType.DMA((8,)), pltpu.SemaphoreType.DMA((8,)),
            pltpu.SemaphoreType.DMA((4,)), pltpu.SemaphoreType.DMA((4,)),
            pltpu.SemaphoreType.DMA((6,)), pltpu.SemaphoreType.DMA((6,)),
        ],
        compiler_params=pltpu.CompilerParams(collective_id=0, has_side_effects=True, vmem_limit_bytes=40 << 20),
    )(
        displacement.reshape(COMP, 4, 8, 128),
        body_force.reshape(COMP, 4, 8, 128),
        stiffness,
        wet_cell,
        wet_normal,
        route.reshape(1, SLOTS),
        tile_u,
        tile_v,
        tile_row.reshape(1, TILES),
        tile_col.reshape(1, TILES),
        tile_rank.reshape(1, TILES),
    )
    return updated.reshape(displacement.shape), pressure, wet


def solution(mesh):
    return jax.shard_map(
        shards,
        mesh=mesh,
        in_specs=(
            P(None, None, "vol", "rep", None),
            P(None, None, "vol", "rep", None),
            P("vol", "rep", None),
            P(("vol", "rep"), None),
            P(None, ("vol", "rep")),
            P(("vol", "rep"), None),
            P(("vol", "rep"), None, None),
            P(("vol", "rep"), None, None),
            P(("vol", "rep")),
            P(("vol", "rep")),
            P(("vol", "rep")),
        ),
        out_specs=(
            P(None, None, "vol", "rep", None),
            P(None, ("vol", "rep")),
            P(None, ("vol", "rep")),
        ),
        check_vma=False,
    )
```

time: 474 us -> 60.9 us (0.13)
  blocking collectives: 253 us -> 0 us
  starting transfers between devices: 91.4 us -> 0 us
  waiting for transfers between devices: 58.2 us -> 0 us
  Pallas kernels: 0 us -> 52.6 us
  local copies, waits for them, and re-layouts: 42.2 us -> 7.19 us
  between operations: 14.4 us -> 0.7 us
  other arithmetic: 12.4 us -> 0 us
    all_gather x1 -> x0, blocking collectives: 253 us -> none  [shards(): surface = lax.all_gather(received, 'vol', axis=1, tiled=True)]
    pallas_call x0 -> x1, Pallas kernels: none -> 52.6 us  [shards(): pl.pallas_call(body, out_shape=(jax.ShapeDtypeStruct((COMP, 4, 8, 128), F...]
    all_to_all x2 -> x0, starting transfers between devices: 48.4 us -> none  [the longest x1 33.3 us: shards(): lax.all_to_all(packed, 'vol', split_axis=1, concat_axis=1, tiled=True)]
    ppermute x16 -> x0, starting transfers between devices: 42.9 us -> none  [the longest x8 26.5 us: with_halo(): lax.ppermute(tail, axis, [(i, (i + 1) % count) for i in range(ends)])]
    all_to_all x2 -> x0, waiting for transfers between devices: 24.8 us -> none  [the longest x1 14.5 us: shards(): lax.all_to_all(packed, 'vol', split_axis=1, concat_axis=1, tiled=True)]
    unnamed x2 -> x0, waiting for transfers between devices: 19.6 us -> none
    ppermute x16 -> x0, waiting for transfers between devices: 13.9 us -> none  [the longest x8 13.8 us: with_halo(): lax.ppermute(head, axis, [((i + 1) % count, i) for i in range(ends)])]
    scatter x1 -> x0, local copies, waits for them, and re-layouts: 12.6 us -> none  [shards(): load.at[:, :, wet_cells]]
  transfers between devices with their start and end apart: 19 -> 0, of which waited for: 8 -> 0; matrix products, arithmetic and copies ran while one was open for 7% -> 0% of each run, Pallas kernels for 0% -> 0%
where the time goes in v1:
time: 60.9 us; the launch traced here: 60.5 us
  Pallas kernels  52.6 us (86%)
  local copies, waits for them, and re-layouts  7.19 us (12%)
  between operations  0.7 us (1%)
    pallas_call x1, Pallas kernels, shards(): pl.pallas_call(body, out_shape=(jax.ShapeDtypeStruct((COMP, 4, 8, 128), F...  52.6 us
    unnamed x25, local copies, waits for them, and re-layouts  7.19 us

profile of v1, /device:TPU:1, one launch (start us, length us, event | category | flops | bytes accessed | tf_op | source)
XLA Modules:
  0.0 60.5 jit_solution(17608700707774752215)
XLA Ops:
  0.6 0.0 copy-start.9
  0.6 0.0 copy-start.10
  0.7 0.0 copy-start.5
  0.7 0.0 copy-start.6
  0.7 0.0 copy-start.7
  0.7 0.0 copy-start.8
  0.7 0.6 copy-done.9
  1.3 0.0 copy-done.10
  1.3 0.0 copy-done.5
  1.3 0.0 copy-done.6
  1.4 0.0 copy-done.7
  1.4 0.0 copy-done.8
  1.4 0.0 copy-start
  1.4 1.0 %copy-done = bf16[32,32,256]{2,1,0:T(8,128)(2,1)S(1)} copy-done((bf16[32,32,256]{2,1,0:T(8,128)(2,1)S(1)}, bf16[32,32,256]{2,1,0:T(8,128)(2,1)}, u32[]{:S(2)}) %copy-start) | copy-done | bytes 524312
  2.4 0.0 copy-start.1
  2.4 1.0 %copy-done.1 = bf16[32,32,256]{2,1,0:T(8,128)(2,1)S(1)} copy-done((bf16[32,32,256]{2,1,0:T(8,128)(2,1)S(1)}, bf16[32,32,256]{2,1,0:T(8,128)(2,1)}, u32[]{:S(2)}) %copy-start.1) | copy-done | bytes 524312
  3.5 0.0 copy-start.2
  3.5 0.9 %copy-done.2 = f32[3,4,4,8,128]{4,3,2,1,0:T(8,128)S(1)} copy-done((f32[3,4,4,8,128]{4,3,2,1,0:T(8,128)S(1)}, f32[3,4,4,8,128]{4,3,2,1,0:T(8,128)}, u32[]{:S(2)}) %copy-start.2) | copy-done | bytes 196632
  4.4 0.0 copy-start.3
  4.4 0.9 %copy-done.3 = f32[3,4,4,8,128]{4,3,2,1,0:T(8,128)S(1)} copy-done((f32[3,4,4,8,128]{4,3,2,1,0:T(8,128)S(1)}, f32[3,4,4,8,128]{4,3,2,1,0:T(8,128)}, u32[]{:S(2)}) %copy-start.3) | copy-done | bytes 196632
  5.3 0.0 copy-start.4
  5.3 0.7 %copy-done.4 = f32[4,8,128]{2,1,0:T(8,128)S(1)} copy-done((f32[4,8,128]{2,1,0:T(8,128)S(1)}, f32[4,8,128]{2,1,0:T(8,128)}, u32[]{:S(2)}) %copy-start.4) | copy-done | bytes 16408
  6.0 52.6 %shard_map.130 = (f32[12,4,8,128]{3,2,1,0:T(8,128)S(1)}, f32[4,256]{1,0:T(4,128)S(1)}, f32[4,128]{1,0:T(4,128)S(1)}) custom-call(f32[12,4,8,128]{3,2,1,0:T(8,128)S(1)} %bitcast.8, f32[12,4,8,128]{3,2,1,0:T(8,128)S(1)} %bitcast.9, f32[4,8,128]{2,1,0:T(8,128)S(1)} %copy-done.4, s32[1,128]{1,0:T(1,128)S(1)} %copy-done.6, f32[3,128]{1,0:T(4,128)S(1)} %copy-done.5, ...), custom_call_target="tpu_custom_call" | custom-call | tf_op jit(solution)/shard_map/pallas_call | solution.py:402
  58.7 0.7 %copy.17 = f32[3,4,4,8,128]{4,3,2,1,0:T(8,128)} copy(f32[3,4,4,8,128]{4,3,2,1,0:T(8,128)S(1)} %bitcast.7) | data formatting | bytes 393216
  59.4 0.6 copy.18
  59.9 0.6 copy.19
Async XLA Ops:
  0.6 0.7 %copy-start.9 = (s32[32]{0:T(128)S(1)}, s32[32]{0:T(128)}, u32[]{:S(2)}) copy-start(s32[32]{0:T(128)} %param.20) | copy-start | bytes 388
  0.6 0.7 %copy-start.10 = (s32[32]{0:T(128)S(1)}, s32[32]{0:T(128)}, u32[]{:S(2)}) copy-start(s32[32]{0:T(128)} %param.21) | copy-start | bytes 388
  0.7 0.7 %copy-start.5 = (f32[3,128]{1,0:T(4,128)S(1)}, f32[3,128]{1,0:T(4,128)}, u32[]{:S(2)}) copy-start(f32[3,128]{1,0:T(4,128)} %wnorm.1) | copy-start | bytes 4612
  0.7 0.7 %copy-start.6 = (s32[1,128]{1,0:T(1,128)S(1)}, s32[1,128]{1,0:T(1,128)}, u32[]{:S(2)}) copy-start(s32[1,128]{1,0:T(1,128)} %wcell.1) | copy-start | bytes 1540
  0.7 0.7 %copy-start.7 = (s32[128,1]{0,1:T(1,128)S(1)}, s32[128,1]{0,1:T(1,128)}, u32[]{:S(2)}) copy-start(s32[128,1]{0,1:T(1,128)} %param.16) | copy-start | bytes 1540
  0.7 0.7 %copy-start.8 = (s32[32]{0:T(128)S(1)}, s32[32]{0:T(128)}, u32[]{:S(2)}) copy-start(s32[32]{0:T(128)} %param.19) | copy-start | bytes 388
  1.4 1.0 %copy-start = (bf16[32,32,256]{2,1,0:T(8,128)(2,1)S(1)}, bf16[32,32,256]{2,1,0:T(8,128)(2,1)}, u32[]{:S(2)}) copy-start(bf16[32,32,256]{2,1,0:T(8,128)(2,1)} %tu_any.1) | copy-start | bytes 1572868
  2.4 1.0 %copy-start.1 = (bf16[32,32,256]{2,1,0:T(8,128)(2,1)S(1)}, bf16[32,32,256]{2,1,0:T(8,128)(2,1)}, u32[]{:S(2)}) copy-start(bf16[32,32,256]{2,1,0:T(8,128)(2,1)} %tv_any.1) | copy-start | bytes 1572868
  3.5 0.9 %copy-start.2 = (f32[3,4,4,8,128]{4,3,2,1,0:T(8,128)S(1)}, f32[3,4,4,8,128]{4,3,2,1,0:T(8,128)}, u32[]{:S(2)}) copy-start(f32[3,4,4,8,128]{4,3,2,1,0:T(8,128)} %param.11) | copy-start | bytes 589828
  4.4 0.9 %copy-start.3 = (f32[3,4,4,8,128]{4,3,2,1,0:T(8,128)S(1)}, f32[3,4,4,8,128]{4,3,2,1,0:T(8,128)}, u32[]{:S(2)}) copy-start(f32[3,4,4,8,128]{4,3,2,1,0:T(8,128)} %param.12) | copy-start | bytes 589828
  5.3 0.7 %copy-start.4 = (f32[4,8,128]{2,1,0:T(8,128)S(1)}, f32[4,8,128]{2,1,0:T(8,128)}, u32[]{:S(2)}) copy-start(f32[4,8,128]{2,1,0:T(8,128)} %stiff.1) | copy-start | bytes 49156

commit v2 on v1

--- a/solution.py
+++ b/solution.py
@@ -18,6 +18,7 @@
 NHI = NX * NZH
 NLO = NY * NC
 NV = NHI * NLO
+NXY = NX * NLO
 SLOTS = 128
 COMP = 12
 TILES, RANK = 32, 32
@@ -63,12 +64,13 @@
 
 
 def body(
-    disp, force, stiff, wcell, wnorm, route, tu_any, tv_any, trow, tcol, trank,
+    disp_h, force_h, stiff_h, wcell_h, wnorm_h, route_h, tu_h, tv_h, trow_h, tcol_h, trank_h,
     out_u, out_p, out_w,
-    tu, tv, vol_s, vol_r, rep_s, rep_r, cor_s, cor_r, fvol_s, fvol_r, frep_s, frep_r,
+    disp, force, stiff, wcell, wnorm, route, tu, tv, trow, tcol, trank,
+    vol_s, vol_r, rep_s, rep_r, cor_s, cor_r, fvol_s, fvol_r, frep_s, frep_r,
     w_ext, f_ext, c_ext, field, base, scale,
-    vdt, ud, ol, rowhot, armask, place, sel_t, diag_m, row_m, sel_lo, lo_hot, ha_hot,
-    ra, g, zs, zr, xb, ws, wr,
+    vdt, ud, ol, rowhot, armask, place, sel_t, diag_m, row_m, sel_at, at_hot, za_hot,
+    ra, g, zs, zr, ws, wr,
     load_sem, halo_ss, halo_rs, fhalo_ss, fhalo_rs, ph_ss, ph_rs,
 ):
     v = lax.axis_index("vol")
@@ -83,9 +85,12 @@
     hi_peers = [(lax.rem(hi + j, NHI) * NLO + lo, r) for j in range(1, NHI)]
     y_peers = [(vol_of(x, zh, lax.rem(y + j, NY), c), r) for j in range(1, NY)]
     core_peer = (vol_of(x, zh, y, 1 - c), r)
-    lo_at = [lax.rem(lo + j, NLO) for j in range(1, NLO)]
-    lo_peers = [(hi * NLO + at, r) for at in lo_at]
-    x_peers = [(vol_of(lax.rem(x + j, NX), zh, y, c), r) for j in range(1, NX)]
+    here = x * NLO + lo
+
+    def plane_peer(j):
+        at = lax.rem(here + j, NXY)
+        return at, (at // NLO * (NZH * NLO) + zh * NLO + lax.rem(at, NLO), r)
+
     z_at = [(zh, lax.rem(r + j, NR)) for j in range(1, NR)] + [(1 - zh, lax.rem(r + j, NR)) for j in range(NR)]
     z_peers = [(vol_of(x, zh_, y, c), r_) for zh_, r_ in z_at]
     up_v, down_v = lax.rem(v + 1, NV), lax.rem(v + NV - 1, NV)
@@ -93,14 +98,17 @@
     halo_peers = [(up_v, r), (down_v, r)] + [(a, b) for a in (up_v, down_v) for b in (up_r, down_r)]
 
     barrier = pltpu.get_barrier_semaphore()
-    greeted = hi_peers + lo_peers + z_peers + halo_peers
+    greeted = halo_peers + z_peers + hi_peers + y_peers + [core_peer]
     for peer in greeted:
         pl.semaphore_signal(barrier, inc=1, device_id=peer, device_id_type=MESH)
 
-    load_u = pltpu.make_async_copy(tu_any, tu, load_sem.at[0])
-    load_v = pltpu.make_async_copy(tv_any, tv, load_sem.at[1])
-    load_u.start()
-    load_v.start()
+    sources = (disp_h, force_h, stiff_h, wcell_h, wnorm_h, route_h, trow_h, tcol_h, trank_h, tv_h, tu_h)
+    targets = (disp, force, stiff, wcell, wnorm, route, trow, tcol, trank, tv, tu)
+    loads = [pltpu.make_async_copy(a, b, load_sem.at[i]) for i, (a, b) in enumerate(zip(sources, targets))]
+    for load in loads:
+        load.start()
+    for load in loads[:3]:
+        load.wait()
 
     row3 = iota((COMP, 4, 8, 128), 2)
     row_c = iota((COMP, 8, 128), 1)
@@ -154,6 +162,8 @@
         def _():
             remote(src, dst, halo_ss.at[at], halo_rs.at[at], dev).start()
 
+    for load in loads[3:]:
+        load.wait()
     route_row = route[...]
     route_sq = jnp.broadcast_to(route_row, (SLOTS, SLOTS))
     route_col = jnp.transpose(route_sq.astype(F32)).astype(I32)
@@ -168,12 +178,14 @@
     ol[0:128] = z_one
     ol[128:256] = z_one
     rowhot[...] = jnp.where(iota((32, SLOTS), 0) == jnp.broadcast_to(cell // 128, (32, SLOTS)), 1.0, 0.0)
-    lo_t = jnp.where(sub == jnp.broadcast_to(lax.rem(route_row, NLO), (SLOTS, SLOTS)), 1.0, 0.0)
-    lo_hot[...] = jnp.transpose(lo_t).astype(BF16)
-    ha = route_row // NLO * 2 + arrival
-    ha_t = jnp.where(sub // 4 == jnp.broadcast_to(ha, (SLOTS, SLOTS)), 1.0, 0.0)
-    ha_hot[...] = jnp.transpose(ha_t)
-    sel_lo[...] = onehot(iota((NLO, NV), 1) == iota((NLO, NV), 0) + hi * NLO)
+    owner_at = route_row // (NZH * NLO) * NLO + lax.rem(route_row, NLO)
+    at_t = jnp.where(sub == jnp.broadcast_to(owner_at, (SLOTS, SLOTS)), 1.0, 0.0)
+    at_hot[...] = jnp.transpose(at_t).astype(BF16)
+    za = lax.rem(route_row // NLO, NZH) * 2 + arrival
+    za_t = jnp.where(sub // 4 == jnp.broadcast_to(za, (SLOTS, SLOTS)), 1.0, 0.0)
+    za_hot[...] = jnp.transpose(za_t)
+    at_row = iota((NXY, NV), 0)
+    sel_at[...] = onehot(iota((NXY, NV), 1) == at_row // NLO * (NZH * NLO) + zh * NLO + lax.rem(at_row, NLO))
 
     spread = onehot(iota((TILES, TQ), 1) // RANK == iota((TILES, TQ), 0))
     lists = jnp.concatenate([jnp.broadcast_to(trank[...], (4, TILES)), jnp.broadcast_to(trow[...], (4, TILES))], axis=0)
@@ -186,8 +198,6 @@
     col_t = jnp.concatenate([col_t, jnp.zeros((128, 96), F32)], axis=1)
     sel_t[...] = jnp.transpose(col_t)[0:TILES].astype(BF16)
 
-    load_v.wait()
-    load_u.wait()
     at_b, at_g = iota((256, 256), 0), iota((256, 256), 1)
     source = lax.rem(at_b // 2, 8) * 32 + lax.rem(at_b // 16, 8) * 4 + at_b // 128 * 2 + lax.rem(at_b, 2)
     perm_v = onehot(at_g == source)
@@ -249,7 +259,7 @@
         field[i] = w[:, 0:8]
         return carry
 
-    lax.fori_loop(0, COMP, sweeps, 0)
+    lax.fori_loop(0, COMP, sweeps, 0, unroll=12)
 
     flat = field[...].reshape(COMP * 32, 128)
     upper = flat.astype(BF16)
@@ -264,6 +274,21 @@
     ra[hi] = message
     for peer in hi_peers:
         remote(ra.at[hi], ra.at[hi], ph_ss.at[0], ph_rs.at[0], peer).start()
+
+    to_row, from_row = iota((64, 64), 0), iota((64, 64), 1)
+    wanted = lax.rem(to_row, 16) // 2 * 8 + lax.rem(to_row, 2) * 4 + to_row // 16
+    reorder = onehot(from_row == wanted)
+
+    def wait_all(region, at, peer):
+        remote(region, region, ph_ss.at[at], ph_rs.at[at], peer).wait_recv()
+
+    wait_all(ra.at[pl.ds(0, NHI - 1)], 0, hi_peers[0])
+    mine = dot(reorder, ra[...].reshape(64, 128).astype(BF16)).astype(BF16).reshape(4, 16, 128)
+    g[c, y] = mine
+    for peer in y_peers:
+        remote(g.at[c, y], g.at[c, y], ph_ss.at[1], ph_rs.at[1], peer).start()
+    wait_all(g.at[c, pl.ds(0, NY - 1)], 1, y_peers[0])
+    remote(g.at[c], g.at[c], ph_ss.at[2], ph_rs.at[2], core_peer).start()
 
     row_f = iota((COMP, 8, 128), 1)
     fvol_s[0] = pairs(field[:, 3])
@@ -288,25 +313,6 @@
         def _():
             dst[...] = jnp.zeros(dst.shape, BF16)
 
-    to_row, from_row = iota((64, 64), 0), iota((64, 64), 1)
-    wanted = lax.rem(to_row, 16) // 2 * 8 + lax.rem(to_row, 2) * 4 + to_row // 16
-    reorder = onehot(from_row == wanted)
-
-    def wait_all(region, at, peer):
-        remote(region, region, ph_ss.at[at], ph_rs.at[at], peer).wait_recv()
-
-    wait_all(ra.at[pl.ds(0, NHI - 1)], 0, hi_peers[0])
-    mine = dot(reorder, ra[...].reshape(64, 128).astype(BF16)).astype(BF16).reshape(4, 16, 128)
-    g[c, y] = mine
-    for peer in y_peers:
-        remote(g.at[c, y], g.at[c, y], ph_ss.at[1], ph_rs.at[1], peer).start()
-    wait_all(g.at[c, pl.ds(0, NY - 1)], 1, y_peers[0])
-    remote(g.at[c], g.at[c], ph_ss.at[2], ph_rs.at[2], core_peer).start()
-
-    for src, dst, at, dev, sends, comes in fmoves:
-        @pl.when(comes)
-        def _():
-            remote(src, dst, fhalo_ss.at[at], fhalo_rs.at[at], dev).wait_recv()
 
     wait_all(g.at[c], 2, core_peer)
 
@@ -325,6 +331,28 @@
     for (zh_, r_), peer in zip(z_at, z_peers):
         remote(zs.at[r_], zr.at[mine_at], ph_ss.at[3], ph_rs.at[3], peer).start()
     zr[mine_at] = zs[r]
+
+    wait_all(zr.at[pl.ds(0, 2 * NR - 1)], 3, z_peers[0])
+    sums = jnp.sum(zr[...].reshape(NZH, NR, 8, 128), axis=1)
+    back = jnp.concatenate([sums.reshape(16, 128), jnp.zeros((112, 128), F32)], axis=0).astype(BF16)
+    ws[...] = dot_nt(sel_at[...], back).reshape(NXY, 1, 128)
+
+    def give_back(j, carry):
+        at, peer = plane_peer(j)
+        remote(ws.at[at], wr.at[here], ph_ss.at[4], ph_rs.at[4], peer).start()
+        return carry
+
+    lax.fori_loop(1, NXY, give_back, 0)
+    wr[here] = ws[here]
+    own = jnp.where(zh == 0, sums[0], sums[1])
+    wide = jnp.concatenate([own[0:4], own[4:8]], axis=1)
+    join = jnp.where(at_g == lax.rem(at_b, 128) * 2 + at_b // 128, 1.0, 0.0)
+    out_p[...] = jnp.dot(wide, join, precision=lax.Precision.HIGHEST, preferred_element_type=F32)
+
+    for src, dst, at, dev, sends, comes in fmoves:
+        @pl.when(comes)
+        def _():
+            remote(src, dst, fhalo_ss.at[at], fhalo_rs.at[at], dev).wait_recv()
 
     low_f, high_f = unpairs(fvol_r[0], (COMP,)), unpairs(fvol_r[1], (COMP,))
     low_y, high_y = unpairs(frep_r[0], (COMP,)), unpairs(frep_r[1], (COMP,))
@@ -340,28 +368,11 @@
         total = total + jnp.where(lane_f == 127, 0.0, pltpu.roll(w, 127, 2))
         base[:, p] = keep * w + f_ext[:, 2 + p, 0:8] + c_ext[2 + p, 0:8][None] * total
 
-    wait_all(zr.at[pl.ds(0, 2 * NR - 1)], 3, z_peers[0])
-    sums = jnp.sum(zr[...].reshape(NZH, NR, 8, 128), axis=1)
-    xb[x] = sums.reshape(16, 128).astype(BF16)
-    for peer in x_peers:
-        remote(xb.at[x], xb.at[x], ph_ss.at[4], ph_rs.at[4], peer).start()
-    own = jnp.where(zh == 0, sums[0], sums[1])
-    wide = jnp.concatenate([own[0:4], own[4:8]], axis=1)
-    join = jnp.where(at_g == lax.rem(at_b, 128) * 2 + at_b // 128, 1.0, 0.0)
-    out_p[...] = jnp.dot(wide, join, precision=lax.Precision.HIGHEST, preferred_element_type=F32)
-
-    wait_all(xb.at[pl.ds(0, NX - 1)], 4, x_peers[0])
-    gathered = xb[...].reshape(64, 128)
-    gathered = jnp.concatenate([gathered, jnp.zeros((64, 128), BF16)], axis=0)
-    ws[...] = dot_nt(sel_lo[...], gathered).reshape(NLO, 1, 128)
-    for at, peer in zip(lo_at, lo_peers):
-        remote(ws.at[at], wr.at[lo], ph_ss.at[5], ph_rs.at[5], peer).start()
-    wr[lo] = ws[lo]
-    wait_all(wr.at[pl.ds(0, NLO - 1)], 5, lo_peers[0])
-
-    got = wr[...].reshape(NLO, 128).astype(BF16)
-    got = jnp.concatenate([got, jnp.zeros((128 - NLO, 128), BF16)], axis=0)
-    per_slot = (dot(lo_hot[...], got) * ha_hot[...]).astype(BF16)
+    wait_all(wr.at[pl.ds(0, NXY - 1)], 4, core_peer)
+
+    got = wr[...].reshape(NXY, 128).astype(BF16)
+    got = jnp.concatenate([got, jnp.zeros((128 - NXY, 128), BF16)], axis=0)
+    per_slot = (dot(at_hot[...], got) * za_hot[...]).astype(BF16)
     wave = onehot(lax.rem(iota((8, 128), 1), 4) == iota((8, 128), 0))
     wet = dot_nt(wave, per_slot)[0:4]
     out_w[...] = wet
@@ -391,13 +402,12 @@
     sent(g.at[c, pl.ds(0, NY - 1)], 1, y_peers[0])
     sent(g.at[c], 2, core_peer)
     sent(zr.at[pl.ds(0, 2 * NR - 1)], 3, z_peers[0])
-    sent(xb.at[pl.ds(0, NX - 1)], 4, x_peers[0])
-    sent(wr.at[pl.ds(0, NLO - 1)], 5, lo_peers[0])
+    sent(wr.at[pl.ds(0, NXY - 1)], 4, core_peer)
 
 
 def shards(displacement, body_force, stiffness, wet_cell, wet_normal, route, tile_u, tile_v, tile_row, tile_col, tile_rank):
     vmem = pl.BlockSpec(memory_space=pltpu.VMEM)
-    anywhere = pl.BlockSpec(memory_space=pl.ANY)
+    hbm = pl.BlockSpec(memory_space=pltpu.HBM)
     V = pltpu.VMEM
     updated, pressure, wet = pl.pallas_call(
         body,
@@ -406,10 +416,13 @@
             jax.ShapeDtypeStruct((4, 256), F32),
             jax.ShapeDtypeStruct((4, SLOTS), F32),
         ),
-        in_specs=[vmem] * 6 + [anywhere] * 2 + [vmem] * 3,
+        in_specs=[hbm] * 11,
         out_specs=(vmem, vmem, vmem),
         scratch_shapes=[
+            V((COMP, 4, 8, 128), F32), V((COMP, 4, 8, 128), F32), V((4, 8, 128), F32),
+            V((1, SLOTS), I32), V((3, SLOTS), F32), V((1, SLOTS), I32),
             V((TILES, RANK, 256), BF16), V((TILES, RANK, 256), BF16),
+            V((1, TILES), I32), V((1, TILES), I32), V((1, TILES), I32),
             V((2, 31, 16, 128), BF16), V((2, 31, 16, 128), BF16),
             V((2, 26, 16, 128), BF16), V((2, 26, 16, 128), BF16),
             V((2, 2, 6, 16, 128), BF16), V((2, 2, 6, 16, 128), BF16),
@@ -419,16 +432,16 @@
             V((COMP, 4, 8, 128), F32), V((COMP, 4, 8, 128), F32), V((4, 8, 128), F32),
             V((256, TQ), BF16), V((TQ, 256), BF16), V((256, SLOTS), BF16), V((32, SLOTS), F32),
             V((8, SLOTS), F32), V((128, SLOTS), BF16), V((TILES, 128), BF16), V((TILES, TQ), F32),
-            V((32, TQ), F32), V((NLO, NV), BF16), V((SLOTS, 128), BF16), V((SLOTS, 128), F32),
+            V((32, TQ), F32), V((NXY, NV), BF16), V((SLOTS, 128), BF16), V((SLOTS, 128), F32),
             V((NHI, 8, 128), F32), V((NC, NY, 4, 16, 128), BF16),
-            V((NR, 8, 128), F32), V((NZH * NR, 8, 128), F32), V((NX, 16, 128), BF16),
-            V((NLO, 1, 128), F32), V((NLO, 1, 128), F32),
-            pltpu.SemaphoreType.DMA((2,)),
+            V((NR, 8, 128), F32), V((NZH * NR, 8, 128), F32),
+            V((NXY, 1, 128), F32), V((NXY, 1, 128), F32),
+            pltpu.SemaphoreType.DMA((11,)),
             pltpu.SemaphoreType.DMA((8,)), pltpu.SemaphoreType.DMA((8,)),
             pltpu.SemaphoreType.DMA((4,)), pltpu.SemaphoreType.DMA((4,)),
-            pltpu.SemaphoreType.DMA((6,)), pltpu.SemaphoreType.DMA((6,)),
+            pltpu.SemaphoreType.DMA((5,)), pltpu.SemaphoreType.DMA((5,)),
         ],
-        compiler_params=pltpu.CompilerParams(collective_id=0, has_side_effects=True, vmem_limit_bytes=40 << 20),
+        compiler_params=pltpu.CompilerParams(collective_id=0, has_side_effects=True, vmem_limit_bytes=56 << 20),
     )(
         displacement.reshape(COMP, 4, 8, 128),
         body_force.reshape(COMP, 4, 8, 128),

time: 60.9 us -> 53.6 us (0.88)
  local copies, waits for them, and re-layouts: 7.19 us -> 2.86 us
  Pallas kernels: 52.6 us -> 49.9 us
    unnamed x25 -> x7, local copies, waits for them, and re-layouts: 7.19 us -> 2.86 us
    pallas_call x1, Pallas kernels: 52.6 us -> 49.9 us  [shards(): pl.pallas_call(body, out_shape=(jax.ShapeDtypeStruct((COMP, 4, 8, 128), F...]
where the time goes in v2:
time: 53.6 us; the launch traced here: 53.5 us
  Pallas kernels  49.9 us (93%)
  local copies, waits for them, and re-layouts  2.86 us (5%)
  between operations  0.65 us (1%)
    pallas_call x1, Pallas kernels, shards(): pl.pallas_call(body, out_shape=(jax.ShapeDtypeStruct((COMP, 4, 8, 128), F...  49.9 us
    unnamed x7, local copies, waits for them, and re-layouts  2.86 us

profile of v2, /device:TPU:1, one launch (start us, length us, event | category | flops | bytes accessed | tf_op | source)
XLA Modules:
  0.0 53.5 jit_solution(9893321344949792886)
XLA Ops:
  0.6 49.9 %shard_map.130 = (f32[12,4,8,128]{3,2,1,0:T(8,128)}, f32[4,256]{1,0:T(4,128)}, f32[4,128]{1,0:T(4,128)}) custom-call(f32[12,4,8,128]{3,2,1,0:T(8,128)} %bitcast.8, f32[12,4,8,128]{3,2,1,0:T(8,128)} %bitcast.9, f32[4,8,128]{2,1,0:T(8,128)} %stiff_h.1, s32[1,128]{1,0:T(1,128)} %wcell_h.1, f32[3,128]{1,0:T(4,128)} %wnorm_h.1, s32[1,128]{1,0:T(1,128)} %bitcast.10, ...), custom_call_target="tpu_custom_call" | custom-call | tf_op jit(solution)/shard_map/pallas_call | solution.py:412
  50.6 0.0 copy-start
  50.6 1.6 %copy.17 = f32[3,4,4,8,128]{4,3,2,1,0:T(8,128)} copy(f32[3,4,4,8,128]{4,3,2,1,0:T(8,128)} %bitcast.7) | data formatting | bytes 393216
  52.2 0.0 copy-done
  52.2 0.0 copy-start.1
  52.2 0.6 %copy.18 = f32[4,256]{1,0:T(4,128)} copy(f32[4,256]{1,0:T(4,128)S(1)} %copy-done) | data formatting | bytes 8192
  52.8 0.1 copy-done.1
  52.9 0.6 %copy.19 = f32[4,128]{1,0:T(4,128)} copy(f32[4,128]{1,0:T(4,128)S(1)} %copy-done.1) | data formatting | bytes 4096
Async XLA Ops:
  50.6 1.6 %copy-start = (f32[4,256]{1,0:T(4,128)S(1)}, f32[4,256]{1,0:T(4,128)}, u32[]{:S(2)}) copy-start(f32[4,256]{1,0:T(4,128)} %get-tuple-element.13) | copy-start | bytes 12292
  52.2 0.7 %copy-start.1 = (f32[4,128]{1,0:T(4,128)S(1)}, f32[4,128]{1,0:T(4,128)}, u32[]{:S(2)}) copy-start(f32[4,128]{1,0:T(4,128)} %get-tuple-element.14) | copy-start | bytes 6148

commit v3 on v2

--- a/solution.py
+++ b/solution.py
@@ -54,21 +54,12 @@
     return tiles.astype(F32).reshape(*lead, 8, 128)
 
 
-def neighbours(inner, low, high):
-    rows = inner.shape[1]
-    lane = iota(inner.shape, 2)
-    total = low + high
-    total = total + pltpu.roll(inner, 1, 1) + pltpu.roll(inner, rows - 1, 1)
-    total = total + jnp.where(lane == 0, 0.0, pltpu.roll(inner, 1, 2))
-    return total + jnp.where(lane == 127, 0.0, pltpu.roll(inner, 127, 2))
-
-
 def body(
     disp_h, force_h, stiff_h, wcell_h, wnorm_h, route_h, tu_h, tv_h, trow_h, tcol_h, trank_h,
     out_u, out_p, out_w,
     disp, force, stiff, wcell, wnorm, route, tu, tv, trow, tcol, trank,
     vol_s, vol_r, rep_s, rep_r, cor_s, cor_r, fvol_s, fvol_r, frep_s, frep_r,
-    w_ext, f_ext, c_ext, field, base, scale,
+    w_ext, f_ext, c_ext, once_ext, twice_ext, field, base, scale,
     vdt, ud, ol, rowhot, armask, place, sel_t, diag_m, row_m, sel_at, at_hot, za_hot,
     ra, g, zs, zr, ws, wr,
     load_sem, halo_ss, halo_rs, fhalo_ss, fhalo_rs, ph_ss, ph_rs,
@@ -110,26 +101,43 @@
     for load in loads[:3]:
         load.wait()
 
+    keep = 1.0 - relax_factor
     row3 = iota((COMP, 4, 8, 128), 2)
     row_c = iota((COMP, 8, 128), 1)
+    lane_c = iota((COMP, 8, 128), 2)
+
+    def inside(w):
+        total = jnp.where(row_c == 0, 0.0, pltpu.roll(w, 1, 1)) + jnp.where(row_c == 7, 0.0, pltpu.roll(w, 7, 1))
+        return total + jnp.where(lane_c == 0, 0.0, pltpu.roll(w, 1, 2)) + jnp.where(lane_c == 127, 0.0, pltpu.roll(w, 127, 2))
+
+    own_inv = relax_factor / (mass_shift + 6.0 * stiff[...])
+    own_c = own_inv * stiff[...]
+    scale[...] = own_inv
+    c_ext[1:5, 0:8] = own_c
+    f_ext[:, :, 0:8] = force[...] * own_inv[None]
     for side in (0, 1):
-        first = 1 - side
-        vol_s[side, 0:18] = pairs(disp[:, first:first + 3])
-        vol_s[side, 18:30] = pairs(force[:, 2 - 2 * side:4 - 2 * side])
-        vol_s[side, 30:31] = pairs(stiff[2 - 2 * side:4 - 2 * side])
-    force_up = pltpu.roll(force[...].reshape(COMP * 4, 8, 128), 4, 1).reshape(COMP, 4, 8, 128)
+        edge, second, third = (3, 2, 1) if side == 0 else (0, 1, 2)
+        w_e, w_2, f_e = disp[:, edge], disp[:, second], f_ext[:, edge, 0:8]
+        c_e, c_2 = own_c[edge], own_c[second]
+        once = keep * w_e + f_e + c_e[None] * (w_2 + inside(w_e))
+        once_2 = keep * w_2 + f_ext[:, second, 0:8] + c_2[None] * (w_e + disp[:, third] + inside(w_2))
+        twice = f_e + c_e[None] * once_2
+        vol_s[side, 0:6] = pairs(w_e)
+        vol_s[side, 6:12] = pairs(once)
+        vol_s[side, 12:18] = pairs(twice)
+        vol_s[side, 18:19] = pairs(jnp.stack([c_e, c_e * c_2]))
+        up = jnp.where(row_c >= 6, w_e, jnp.where(row_c == 5, pltpu.roll(once, 6, 1), pltpu.roll(w_2, 5, 1)))
+        down = jnp.where(row_c <= 1, w_e, jnp.where(row_c == 2, pltpu.roll(once, 2, 1), pltpu.roll(w_2, 3, 1)))
+        half = row_c[0:6] >= 4
+        cor_s[side, 0, 0:3] = pairs(jnp.where(half, up[6:12], pltpu.roll(up[0:6], 4, 1)))
+        cor_s[side, 1, 0:3] = pairs(jnp.where(half, pltpu.roll(down[6:12], 4, 1), down[0:6]))
+        for t in (0, 1):
+            cor_s[side, t, 3:4] = pairs(jnp.stack([c_e, c_e]))
+    force_up = pltpu.roll(f_ext[:, :, 0:8].reshape(COMP * 4, 8, 128), 4, 1).reshape(COMP, 4, 8, 128)
     rep_s[0, 0:24] = pairs(jnp.where(row3 >= 5, disp[...], force_up))
     rep_s[1, 0:24] = pairs(jnp.where(row3 <= 2, disp[...], force_up))
     for side in (0, 1):
-        rep_s[side, 24:26] = pairs(stiff[...])
-        edge, second = (3, 2) if side == 0 else (0, 1)
-        w_e, w_2, f_e = disp[:, edge], disp[:, second], force[:, edge]
-        s_e = jnp.broadcast_to(stiff[edge:edge + 1], (COMP, 8, 128))
-        w_2 = pltpu.roll(w_2, 4, 1)
-        up = jnp.where(row_c >= 6, w_e, jnp.where(row_c == 3, w_2, jnp.where(row_c == 1, pltpu.roll(f_e, 2, 1), pltpu.roll(s_e, 1, 1))))
-        down = jnp.where(row_c <= 1, w_e, jnp.where(row_c == 4, w_2, jnp.where(row_c == 6, pltpu.roll(f_e, 6, 1), pltpu.roll(s_e, 7, 1))))
-        cor_s[side, 0] = pairs(up)
-        cor_s[side, 1] = pairs(down)
+        rep_s[side, 24:26] = pairs(own_c)
 
     vol_to = [v < NV - 1, v > 0]
     vol_from = [v > 0, v < NV - 1]
@@ -205,58 +213,62 @@
     split = at_b == lax.rem(at_g, 128) * 2 + at_g // 128
     ud[...] = dot(tu[...].reshape(TQ, 256), onehot(split)).astype(BF16)
 
-    w_ext[:, 3:7, 0:8] = disp[...]
-    w_ext[:, 0:1, 8:16] = jnp.zeros((COMP, 1, 8, 128), F32)
-    w_ext[:, 9:10, 8:16] = jnp.zeros((COMP, 1, 8, 128), F32)
-    s_own = stiff[...]
-    own_inv = relax_factor / (mass_shift + 6.0 * s_own)
-    scale[...] = own_inv
-    c_ext[2:6, 0:8] = own_inv * s_own
-    f_ext[:, 2:6, 0:8] = force[...] * own_inv[None]
+    w_ext[:, 1:5, 0:8] = disp[...]
 
     for src, dst, at, dev, sends, comes in moves:
         @pl.when(comes)
         def _():
             remote(src, dst, halo_ss.at[at], halo_rs.at[at], dev).wait_recv()
 
+    low_r, high_r = unpairs(rep_r[0, 0:24], (COMP, 4)), unpairs(rep_r[1, 0:24], (COMP, 4))
+    w_ext[:, 1:5, 8:16] = jnp.where(row3 <= 2, high_r, low_r)
+    f_ext[:, :, 8:16] = pltpu.roll(jnp.where(row3 >= 4, high_r, low_r).reshape(COMP * 4, 8, 128), 4, 1).reshape(COMP, 4, 8, 128)
+    c_ext[1:5, 8:16] = jnp.where(iota((4, 8, 128), 1) <= 3, unpairs(rep_r[1, 24:26], (4,)), unpairs(rep_r[0, 24:26], (4,)))
     for s in (0, 1):
-        w_ext[:, 7 * s:7 * s + 3, 0:8] = unpairs(vol_r[s, 0:18], (COMP, 3))
-        s_v = unpairs(vol_r[s, 30:31], (2,))
-        inv = relax_factor / (mass_shift + 6.0 * s_v)
-        c_ext[6 * s:6 * s + 2, 0:8] = inv * s_v
-        f_ext[:, 6 * s:6 * s + 2, 0:8] = unpairs(vol_r[s, 18:30], (COMP, 2)) * inv[None]
-    low_r, high_r = unpairs(rep_r[0, 0:24], (COMP, 4)), unpairs(rep_r[1, 0:24], (COMP, 4))
-    w_ext[:, 3:7, 8:16] = jnp.where(row3 <= 2, high_r, low_r)
-    s_b = jnp.where(iota((4, 8, 128), 1) <= 3, unpairs(rep_r[1, 24:26], (4,)), unpairs(rep_r[0, 24:26], (4,)))
-    inv = relax_factor / (mass_shift + 6.0 * s_b)
-    c_ext[2:6, 8:16] = inv * s_b
-    f_b = pltpu.roll(jnp.where(row3 >= 4, high_r, low_r).reshape(COMP * 4, 8, 128), 4, 1).reshape(COMP, 4, 8, 128)
-    f_ext[:, 2:6, 8:16] = f_b * inv[None]
-    zero_plane = jnp.zeros((1, 8, 128), F32)
-    for s in (0, 1):
-        low_c, high_c = unpairs(cor_r[s, 0], (COMP,)), unpairs(cor_r[s, 1], (COMP,))
-        near, far = (2, 1) if s == 0 else (7, 8)
-        w_ext[:, near, 8:16] = jnp.where(row_c <= 3, high_c, low_c)
-        w_ext[:, far, 8:16] = jnp.where(row_c <= 3, pltpu.roll(high_c, 4, 1), pltpu.roll(low_c, 4, 1))
-        s_c = jnp.where(row_c[0] <= 3, pltpu.roll(high_c[0], 1, 0), pltpu.roll(low_c[0], 7, 0))
-        s_c = jnp.where(jnp.logical_or(row_c[0] == 0, row_c[0] == 7), s_c, 0.0)
-        f_c = jnp.where(row_c <= 3, pltpu.roll(high_c, 2, 1), pltpu.roll(low_c, 6, 1))
-        inv = relax_factor / (mass_shift + 6.0 * s_c)
-        c_near, c_far = (1, 0) if s == 0 else (6, 7)
-        c_ext[c_near, 8:16] = inv * s_c
-        f_ext[:, c_near, 8:16] = f_c * inv[None]
-        c_ext[c_far:c_far + 1, 8:16] = zero_plane
-        f_ext[:, c_far, 8:16] = jnp.zeros((COMP, 8, 128), F32)
-
-    keep = 1.0 - relax_factor
+        at = 5 * s
+        w_ext[:, at, 0:8] = unpairs(vol_r[s, 0:6], (COMP,))
+        once_ext[:, s, 0:8] = unpairs(vol_r[s, 6:12], (COMP,))
+        c_s = unpairs(vol_r[s, 18:19], (2,))
+        c_ext[at, 0:8] = c_s[0]
+        low_t, high_t = unpairs(cor_r[s, 0, 0:3], (6,)), unpairs(cor_r[s, 1, 0:3], (6,))
+        low_c = jnp.concatenate([pltpu.roll(low_t, 4, 1), low_t], axis=0)
+        high_c = jnp.concatenate([high_t, pltpu.roll(high_t, 4, 1)], axis=0)
+        upper_half = row_c <= 3
+        w_ext[:, at, 8:16] = jnp.where(upper_half, high_c, low_c)
+        once_ext[:, s, 8:16] = jnp.where(upper_half, pltpu.roll(high_c, 6, 1), pltpu.roll(low_c, 2, 1))
+        c_low, c_high = unpairs(cor_r[s, 0, 3:4], (2,)), unpairs(cor_r[s, 1, 3:4], (2,))
+        c_ext[at, 8:16] = jnp.where(upper_half[0], c_high[0], c_low[0])
+        beside = jnp.where(row_c == 0, pltpu.roll(low_c, 4, 1), jnp.where(row_c == 7, pltpu.roll(high_c, 4, 1), 0.0))
+        twice_ext[:, s] = unpairs(vol_r[s, 12:18], (COMP,)) + c_s[1][None] * beside
+
+    row_p = iota((1, 16, 128), 1)
+    first_row = jnp.logical_or(row_p == 0, row_p == 8)
+    last_row = jnp.logical_or(row_p == 7, row_p == 15)
+
+    def across(w):
+        return jnp.where(first_row, pltpu.roll(w, 1, 1), 0.0) + jnp.where(last_row, pltpu.roll(w, 15, 1), 0.0)
+
+    def beside_in_plane(w):
+        lane = iota(w.shape, 2)
+        total = pltpu.roll(w, 1, 1) + pltpu.roll(w, 15, 1)
+        total = total + jnp.where(lane == 0, 0.0, pltpu.roll(w, 1, 2))
+        return total + jnp.where(lane == 127, 0.0, pltpu.roll(w, 127, 2))
 
     def sweeps(i, carry):
-        w = w_ext[i]
-        f, cc = f_ext[i], c_ext[...]
-        w = keep * w[1:9] + f + cc * neighbours(w[1:9], w[0:8], w[2:10])
-        w = keep * w[1:7] + f[1:7] + cc[1:7] * neighbours(w[1:7], w[0:6], w[2:8])
-        w = keep * w[1:5] + f[2:6] + cc[2:6] * neighbours(w[1:5], w[0:4], w[2:6])
-        field[i] = w[:, 0:8]
+        w, f, cc = w_ext[i], f_ext[i], c_ext[...]
+        once, twice = once_ext[i], twice_ext[i]
+        low, high, own = w[0:1], w[5:6], w[1:5]
+        next_own = keep * own + f + cc[1:5] * (w[0:4] + w[2:6] + beside_in_plane(own))
+        low = once[0:1] + cc[0:1] * (own[0:1] + across(low))
+        high = once[1:2] + cc[5:6] * (own[3:4] + across(high))
+        own = next_own
+        w = jnp.concatenate([low, own, high], axis=0)
+        next_own = keep * own + f + cc[1:5] * (w[0:4] + w[2:6] + beside_in_plane(own))
+        low = twice[0:1] + (keep * low + cc[0:1] * (own[0:1] + beside_in_plane(low)))[:, 0:8]
+        high = twice[1:2] + (keep * high + cc[5:6] * (own[3:4] + beside_in_plane(high)))[:, 0:8]
+        own = next_own[:, 0:8]
+        w = jnp.concatenate([low, own, high], axis=0)
+        field[i] = keep * own + f[:, 0:8] + cc[1:5, 0:8] * (w[0:4] + w[2:6] + beside_in_plane(next_own)[:, 0:8])
         return carry
 
     lax.fori_loop(0, COMP, sweeps, 0, unroll=12)
@@ -366,7 +378,7 @@
         lane_f = iota((COMP, 8, 128), 2)
         total = total + jnp.where(lane_f == 0, 0.0, pltpu.roll(w, 1, 2))
         total = total + jnp.where(lane_f == 127, 0.0, pltpu.roll(w, 127, 2))
-        base[:, p] = keep * w + f_ext[:, 2 + p, 0:8] + c_ext[2 + p, 0:8][None] * total
+        base[:, p] = keep * w + f_ext[:, p, 0:8] + c_ext[1 + p, 0:8][None] * total
 
     wait_all(wr.at[pl.ds(0, NXY - 1)], 4, core_peer)
 
@@ -403,6 +415,12 @@
     sent(g.at[c], 2, core_peer)
     sent(zr.at[pl.ds(0, 2 * NR - 1)], 3, z_peers[0])
     sent(wr.at[pl.ds(0, NXY - 1)], 4, core_peer)
+
+
+def hand_out(u, p, w, out_u, out_p, out_w):
+    out_u[...] = u[...]
+    out_p[...] = p[...]
+    out_w[...] = w[...]
 
 
 def shards(displacement, body_force, stiffness, wet_cell, wet_normal, route, tile_u, tile_v, tile_row, tile_col, tile_rank):
@@ -423,12 +441,13 @@
             V((1, SLOTS), I32), V((3, SLOTS), F32), V((1, SLOTS), I32),
             V((TILES, RANK, 256), BF16), V((TILES, RANK, 256), BF16),
             V((1, TILES), I32), V((1, TILES), I32), V((1, TILES), I32),
-            V((2, 31, 16, 128), BF16), V((2, 31, 16, 128), BF16),
+            V((2, 19, 16, 128), BF16), V((2, 19, 16, 128), BF16),
             V((2, 26, 16, 128), BF16), V((2, 26, 16, 128), BF16),
-            V((2, 2, 6, 16, 128), BF16), V((2, 2, 6, 16, 128), BF16),
+            V((2, 2, 4, 16, 128), BF16), V((2, 2, 4, 16, 128), BF16),
             V((2, 6, 16, 128), BF16), V((2, 6, 16, 128), BF16),
             V((2, 6, 16, 128), BF16), V((2, 6, 16, 128), BF16),
-            V((COMP, 10, 16, 128), F32), V((COMP, 8, 16, 128), F32), V((8, 16, 128), F32),
+            V((COMP, 6, 16, 128), F32), V((COMP, 4, 16, 128), F32), V((6, 16, 128), F32),
+            V((COMP, 2, 16, 128), F32), V((COMP, 2, 8, 128), F32),
             V((COMP, 4, 8, 128), F32), V((COMP, 4, 8, 128), F32), V((4, 8, 128), F32),
             V((256, TQ), BF16), V((TQ, 256), BF16), V((256, SLOTS), BF16), V((32, SLOTS), F32),
             V((8, SLOTS), F32), V((128, SLOTS), BF16), V((TILES, 128), BF16), V((TILES, TQ), F32),
@@ -455,6 +474,17 @@
         tile_col.reshape(1, TILES),
         tile_rank.reshape(1, TILES),
     )
+    updated, pressure, wet = pl.pallas_call(
+        hand_out,
+        out_shape=(
+            jax.ShapeDtypeStruct((COMP, 4, 8, 128), F32),
+            jax.ShapeDtypeStruct((4, 256), F32),
+            jax.ShapeDtypeStruct((4, SLOTS), F32),
+        ),
+        in_specs=[vmem] * 3,
+        out_specs=(vmem, vmem, vmem),
+        compiler_params=pltpu.CompilerParams(vmem_limit_bytes=56 << 20),
+    )(updated, pressure, wet)
     return updated.reshape(displacement.shape), pressure, wet
 
 

time: 53.6 us -> 50.2 us (0.937)
  local copies, waits for them, and re-layouts: 2.86 us -> 0 us
    unnamed x7 -> x0, local copies, waits for them, and re-layouts: 2.86 us -> none
    pallas_call x1, Pallas kernels: 49.9 us -> 47.8 us  [shards(): pl.pallas_call(body, out_shape=(jax.ShapeDtypeStruct((COMP, 4, 8, 128), F...]
    pallas_call x0 -> x1, Pallas kernels: none -> 1.63 us  [shards(): pl.pallas_call(hand_out, out_shape=(jax.ShapeDtypeStruct((COMP, 4, 8, 128...]
where the time goes in v3:
time: 50.2 us; the launch traced here: 50 us
  Pallas kernels  49.4 us (98%)
  between operations  0.64 us (1%)
    pallas_call x1, Pallas kernels, shards(): pl.pallas_call(body, out_shape=(jax.ShapeDtypeStruct((COMP, 4, 8, 128), F...  47.8 us
    pallas_call x1, Pallas kernels, shards(): pl.pallas_call(hand_out, out_shape=(jax.ShapeDtypeStruct((COMP, 4, 8, 128...  1.63 us

profile of v3, /device:TPU:1, one launch (start us, length us, event | category | flops | bytes accessed | tf_op | source)
XLA Modules:
  0.0 50.0 jit_solution(813749280727634622)
XLA Ops:
  0.6 47.8 %shard_map.130 = (f32[12,4,8,128]{3,2,1,0:T(8,128)}, f32[4,256]{1,0:T(4,128)}, f32[4,128]{1,0:T(4,128)}) custom-call(f32[12,4,8,128]{3,2,1,0:T(8,128)} %bitcast.7, f32[12,4,8,128]{3,2,1,0:T(8,128)} %bitcast.8, f32[4,8,128]{2,1,0:T(8,128)} %stiff_h.1, s32[1,128]{1,0:T(1,128)} %wcell_h.1, f32[3,128]{1,0:T(4,128)} %wnorm_h.1, s32[1,128]{1,0:T(1,128)} %bitcast.9, ...), custom_call_target="tpu_custom_call" | custom-call | tf_op jit(solution)/shard_map/pallas_call | solution.py:430
  48.4 1.6 %shard_map.131 = (f32[12,4,8,128]{3,2,1,0:T(8,128)}, f32[4,256]{1,0:T(4,128)}, f32[4,128]{1,0:T(4,128)}) custom-call(f32[12,4,8,128]{3,2,1,0:T(8,128)} %get-tuple-element.9.u, f32[4,256]{1,0:T(4,128)} %get-tuple-element.10.p, f32[4,128]{1,0:T(4,128)} %get-tuple-element.11.w), custom_call_target="tpu_custom_call" | custom-call | tf_op jit(solution)/shard_map/pallas_call | solution.py:477

commit v4 on v3

--- a/solution.py
+++ b/solution.py
@@ -59,7 +59,8 @@
     out_u, out_p, out_w,
     disp, force, stiff, wcell, wnorm, route, tu, tv, trow, tcol, trank,
     vol_s, vol_r, rep_s, rep_r, cor_s, cor_r, fvol_s, fvol_r, frep_s, frep_r,
-    w_ext, f_ext, c_ext, once_ext, twice_ext, field, base, scale,
+    alone, f_own, c_own, ring_w, ring_once, ring_twice, ring_c, face_w, face_once, face_twice, face_c,
+    corner_w, corner_once, corner_c, field, base, scale,
     vdt, ud, ol, rowhot, armask, place, sel_t, diag_m, row_m, sel_at, at_hot, za_hot,
     ra, g, zs, zr, ws, wr,
     load_sem, halo_ss, halo_rs, fhalo_ss, fhalo_rs, ph_ss, ph_rs,
@@ -89,7 +90,7 @@
     halo_peers = [(up_v, r), (down_v, r)] + [(a, b) for a in (up_v, down_v) for b in (up_r, down_r)]
 
     barrier = pltpu.get_barrier_semaphore()
-    greeted = halo_peers + z_peers + hi_peers + y_peers + [core_peer]
+    greeted = halo_peers + hi_peers + z_peers + y_peers + [core_peer]
     for peer in greeted:
         pl.semaphore_signal(barrier, inc=1, device_id=peer, device_id_type=MESH)
 
@@ -102,42 +103,82 @@
         load.wait()
 
     keep = 1.0 - relax_factor
-    row3 = iota((COMP, 4, 8, 128), 2)
+
+    def rolled(w, shift, axis):
+        shift = shift % (8 if axis == w.ndim - 2 else 128)
+        if shift == 0:
+            return w
+        return pltpu.roll(w.reshape(-1, 8, 128), shift, axis - w.ndim + 3).reshape(w.shape)
+
+    def sides(w, ring):
+        row = iota(w.shape, w.ndim - 2)
+        axis = w.ndim - 2
+        before, after = rolled(ring, 1, axis), rolled(ring, 7, axis)
+        return jnp.where(row == 0, before, rolled(w, 1, axis)) + jnp.where(row == 7, after, rolled(w, 7, axis))
+
+    def from_ring(ring):
+        row = iota(ring.shape, ring.ndim - 2)
+        axis = ring.ndim - 2
+        return jnp.where(row == 0, rolled(ring, 1, axis), jnp.where(row == 7, rolled(ring, 7, axis), 0.0))
+
+    def to_ring(w):
+        row = iota(w.shape, w.ndim - 2)
+        axis = w.ndim - 2
+        return jnp.where(row == 0, rolled(w, 1, axis), rolled(w, 7, axis))
+
+    def along_z(w):
+        lane = iota(w.shape, w.ndim - 1)
+        axis = w.ndim - 1
+        return jnp.where(lane == 0, 0.0, rolled(w, 1, axis)) + jnp.where(lane == 127, 0.0, rolled(w, 127, axis))
+
     row_c = iota((COMP, 8, 128), 1)
-    lane_c = iota((COMP, 8, 128), 2)
-
-    def inside(w):
-        total = jnp.where(row_c == 0, 0.0, pltpu.roll(w, 1, 1)) + jnp.where(row_c == 7, 0.0, pltpu.roll(w, 7, 1))
-        return total + jnp.where(lane_c == 0, 0.0, pltpu.roll(w, 1, 2)) + jnp.where(lane_c == 127, 0.0, pltpu.roll(w, 127, 2))
-
     own_inv = relax_factor / (mass_shift + 6.0 * stiff[...])
     own_c = own_inv * stiff[...]
     scale[...] = own_inv
-    c_ext[1:5, 0:8] = own_c
-    f_ext[:, :, 0:8] = force[...] * own_inv[None]
+    c_own[...] = own_c
+    f_own[...] = force[...] * own_inv[None]
+    for p in range(4):
+        w = disp[:, p]
+        total = sides(w, jnp.zeros_like(w)) + along_z(w)
+        if p > 0:
+            total = total + disp[:, p - 1]
+        if p < 3:
+            total = total + disp[:, p + 1]
+        alone[:, p] = keep * w + f_own[:, p] + own_c[p][None] * total
+
+    def row_of_planes(plane, row, start):
+        out = None
+        for p in range(4):
+            moved = rolled(plane(p), start + p - row, 1)
+            out = moved if out is None else jnp.where(iota(moved.shape, 1) == start + p, moved, out)
+        return out
+
     for side in (0, 1):
-        edge, second, third = (3, 2, 1) if side == 0 else (0, 1, 2)
-        w_e, w_2, f_e = disp[:, edge], disp[:, second], f_ext[:, edge, 0:8]
-        c_e, c_2 = own_c[edge], own_c[second]
-        once = keep * w_e + f_e + c_e[None] * (w_2 + inside(w_e))
-        once_2 = keep * w_2 + f_ext[:, second, 0:8] + c_2[None] * (w_e + disp[:, third] + inside(w_2))
-        twice = f_e + c_e[None] * once_2
+        edge, second = (3, 2) if side == 0 else (0, 1)
+        w_e, w_2, once = disp[:, edge], disp[:, second], alone[:, edge]
+        c_e = own_c[edge]
         vol_s[side, 0:6] = pairs(w_e)
         vol_s[side, 6:12] = pairs(once)
-        vol_s[side, 12:18] = pairs(twice)
-        vol_s[side, 18:19] = pairs(jnp.stack([c_e, c_e * c_2]))
-        up = jnp.where(row_c >= 6, w_e, jnp.where(row_c == 5, pltpu.roll(once, 6, 1), pltpu.roll(w_2, 5, 1)))
-        down = jnp.where(row_c <= 1, w_e, jnp.where(row_c == 2, pltpu.roll(once, 2, 1), pltpu.roll(w_2, 3, 1)))
+        vol_s[side, 12:18] = pairs(f_own[:, edge] + c_e[None] * alone[:, second])
+        vol_s[side, 18:19] = pairs(jnp.stack([c_e, c_e * own_c[second]]))
+        up = jnp.where(row_c >= 6, w_e, jnp.where(row_c == 5, rolled(once, 6, 1), rolled(w_2, 5, 1)))
+        down = jnp.where(row_c <= 1, w_e, jnp.where(row_c == 2, rolled(once, 2, 1), rolled(w_2, 3, 1)))
         half = row_c[0:6] >= 4
-        cor_s[side, 0, 0:3] = pairs(jnp.where(half, up[6:12], pltpu.roll(up[0:6], 4, 1)))
-        cor_s[side, 1, 0:3] = pairs(jnp.where(half, pltpu.roll(down[6:12], 4, 1), down[0:6]))
+        cor_s[side, 0, 0:3] = pairs(jnp.where(half, up[6:12], rolled(up[0:6], 4, 1)))
+        cor_s[side, 1, 0:3] = pairs(jnp.where(half, rolled(down[6:12], 4, 1), down[0:6]))
         for t in (0, 1):
             cor_s[side, t, 3:4] = pairs(jnp.stack([c_e, c_e]))
-    force_up = pltpu.roll(f_ext[:, :, 0:8].reshape(COMP * 4, 8, 128), 4, 1).reshape(COMP, 4, 8, 128)
-    rep_s[0, 0:24] = pairs(jnp.where(row3 >= 5, disp[...], force_up))
-    rep_s[1, 0:24] = pairs(jnp.where(row3 <= 2, disp[...], force_up))
-    for side in (0, 1):
-        rep_s[side, 24:26] = pairs(own_c)
+        row, inner = (7, 1) if side == 0 else (0, 7)
+        first = row_of_planes(lambda p: disp[:, p], row, 0)
+        then = row_of_planes(lambda p: alone[:, p], row, 4)
+        rep_s[side, 0:6] = pairs(jnp.where(row_c < 4, first, then))
+        last = [row_of_planes(lambda p: f_own[a:a + 6, p] + own_c[p][None] * rolled(alone[a:a + 6, p], inner, 1), row, start)
+                for a, start in ((0, 0), (6, 4))]
+        rep_s[side, 6:9] = pairs(jnp.where(half, last[1], last[0]))
+        c_rows = row_of_planes(lambda p: own_c[p:p + 1], row, 0)
+        cc_rows = row_of_planes(lambda p: own_c[p:p + 1] * rolled(own_c[p:p + 1], inner, 1), row, 4)
+        c_rows = jnp.where(row_c[0:1] < 4, c_rows, cc_rows)
+        rep_s[side, 9:10] = pairs(jnp.concatenate([c_rows, c_rows], axis=0))
 
     vol_to = [v < NV - 1, v > 0]
     vol_from = [v > 0, v < NV - 1]
@@ -207,68 +248,74 @@
     sel_t[...] = jnp.transpose(col_t)[0:TILES].astype(BF16)
 
     at_b, at_g = iota((256, 256), 0), iota((256, 256), 1)
-    source = lax.rem(at_b // 2, 8) * 32 + lax.rem(at_b // 16, 8) * 4 + at_b // 128 * 2 + lax.rem(at_b, 2)
+    source = lax.rem(at_b, 8) * 32 + lax.rem(at_b // 16, 8) * 4 + at_b // 128 * 2 + lax.rem(at_b // 8, 2)
     perm_v = onehot(at_g == source)
     vdt[...] = dot_nt(perm_v, tv[...].reshape(TQ, 256)).astype(BF16)
     split = at_b == lax.rem(at_g, 128) * 2 + at_g // 128
     ud[...] = dot(tu[...].reshape(TQ, 256), onehot(split)).astype(BF16)
 
-    w_ext[:, 1:5, 0:8] = disp[...]
-
     for src, dst, at, dev, sends, comes in moves:
         @pl.when(comes)
         def _():
             remote(src, dst, halo_ss.at[at], halo_rs.at[at], dev).wait_recv()
 
-    low_r, high_r = unpairs(rep_r[0, 0:24], (COMP, 4)), unpairs(rep_r[1, 0:24], (COMP, 4))
-    w_ext[:, 1:5, 8:16] = jnp.where(row3 <= 2, high_r, low_r)
-    f_ext[:, :, 8:16] = pltpu.roll(jnp.where(row3 >= 4, high_r, low_r).reshape(COMP * 4, 8, 128), 4, 1).reshape(COMP, 4, 8, 128)
-    c_ext[1:5, 8:16] = jnp.where(iota((4, 8, 128), 1) <= 3, unpairs(rep_r[1, 24:26], (4,)), unpairs(rep_r[0, 24:26], (4,)))
+    upper_half = row_c <= 3
+
+    def ring_of(low, high, start):
+        return [jnp.where(iota(low.shape, 1) <= 3, rolled(high, -start - p, 1), rolled(low, 7 - start - p, 1)) for p in range(4)]
+
+    low_r, high_r = unpairs(rep_r[0, 0:6], (COMP,)), unpairs(rep_r[1, 0:6], (COMP,))
+    for p, (w, once) in enumerate(zip(ring_of(low_r, high_r, 0), ring_of(low_r, high_r, 4))):
+        ring_w[:, p] = w
+        ring_once[:, p] = once
+    low_r, high_r = unpairs(rep_r[0, 6:9], (6,)), unpairs(rep_r[1, 6:9], (6,))
+    for p, (a, b) in enumerate(zip(ring_of(low_r, high_r, 0), ring_of(low_r, high_r, 4))):
+        ring_twice[0:6, p] = a
+        ring_twice[6:12, p] = b
+    low_r, high_r = unpairs(rep_r[0, 9:10], (2,))[0:1], unpairs(rep_r[1, 9:10], (2,))[0:1]
+    ring_cc = ring_of(low_r, high_r, 4)
+    for p, part in enumerate(ring_of(low_r, high_r, 0)):
+        ring_c[p:p + 1] = part
     for s in (0, 1):
-        at = 5 * s
-        w_ext[:, at, 0:8] = unpairs(vol_r[s, 0:6], (COMP,))
-        once_ext[:, s, 0:8] = unpairs(vol_r[s, 6:12], (COMP,))
+        face_w[:, s] = unpairs(vol_r[s, 0:6], (COMP,))
+        face_once[:, s] = unpairs(vol_r[s, 6:12], (COMP,))
         c_s = unpairs(vol_r[s, 18:19], (2,))
-        c_ext[at, 0:8] = c_s[0]
+        face_c[s] = c_s[0]
         low_t, high_t = unpairs(cor_r[s, 0, 0:3], (6,)), unpairs(cor_r[s, 1, 0:3], (6,))
-        low_c = jnp.concatenate([pltpu.roll(low_t, 4, 1), low_t], axis=0)
-        high_c = jnp.concatenate([high_t, pltpu.roll(high_t, 4, 1)], axis=0)
-        upper_half = row_c <= 3
-        w_ext[:, at, 8:16] = jnp.where(upper_half, high_c, low_c)
-        once_ext[:, s, 8:16] = jnp.where(upper_half, pltpu.roll(high_c, 6, 1), pltpu.roll(low_c, 2, 1))
+        low_c = jnp.concatenate([rolled(low_t, 4, 1), low_t], axis=0)
+        high_c = jnp.concatenate([high_t, rolled(high_t, 4, 1)], axis=0)
+        corner_w[:, s] = jnp.where(upper_half, high_c, low_c)
+        corner_once[:, s] = jnp.where(upper_half, rolled(high_c, 6, 1), rolled(low_c, 2, 1))
         c_low, c_high = unpairs(cor_r[s, 0, 3:4], (2,)), unpairs(cor_r[s, 1, 3:4], (2,))
-        c_ext[at, 8:16] = jnp.where(upper_half[0], c_high[0], c_low[0])
-        beside = jnp.where(row_c == 0, pltpu.roll(low_c, 4, 1), jnp.where(row_c == 7, pltpu.roll(high_c, 4, 1), 0.0))
-        twice_ext[:, s] = unpairs(vol_r[s, 12:18], (COMP,)) + c_s[1][None] * beside
-
-    row_p = iota((1, 16, 128), 1)
-    first_row = jnp.logical_or(row_p == 0, row_p == 8)
-    last_row = jnp.logical_or(row_p == 7, row_p == 15)
-
-    def across(w):
-        return jnp.where(first_row, pltpu.roll(w, 1, 1), 0.0) + jnp.where(last_row, pltpu.roll(w, 15, 1), 0.0)
-
-    def beside_in_plane(w):
-        lane = iota(w.shape, 2)
-        total = pltpu.roll(w, 1, 1) + pltpu.roll(w, 15, 1)
-        total = total + jnp.where(lane == 0, 0.0, pltpu.roll(w, 1, 2))
-        return total + jnp.where(lane == 127, 0.0, pltpu.roll(w, 127, 2))
+        corner_c[s] = jnp.where(upper_half[0], c_high[0], c_low[0])
+        beside = jnp.where(row_c == 0, rolled(low_c, 4, 1), jnp.where(row_c == 7, rolled(high_c, 4, 1), 0.0))
+        face_twice[:, s] = unpairs(vol_r[s, 12:18], (COMP,)) + c_s[1][None] * beside
+        below = jnp.where(upper_half, rolled(high_c, 7, 1), rolled(low_c, 1, 1))
+        ring_twice[:, 3 * s] = ring_twice[:, 3 * s] + ring_cc[3 * s] * below
 
     def sweeps(i, carry):
-        w, f, cc = w_ext[i], f_ext[i], c_ext[...]
-        once, twice = once_ext[i], twice_ext[i]
-        low, high, own = w[0:1], w[5:6], w[1:5]
-        next_own = keep * own + f + cc[1:5] * (w[0:4] + w[2:6] + beside_in_plane(own))
-        low = once[0:1] + cc[0:1] * (own[0:1] + across(low))
-        high = once[1:2] + cc[5:6] * (own[3:4] + across(high))
-        own = next_own
-        w = jnp.concatenate([low, own, high], axis=0)
-        next_own = keep * own + f + cc[1:5] * (w[0:4] + w[2:6] + beside_in_plane(own))
-        low = twice[0:1] + (keep * low + cc[0:1] * (own[0:1] + beside_in_plane(low)))[:, 0:8]
-        high = twice[1:2] + (keep * high + cc[5:6] * (own[3:4] + beside_in_plane(high)))[:, 0:8]
-        own = next_own[:, 0:8]
-        w = jnp.concatenate([low, own, high], axis=0)
-        field[i] = keep * own + f[:, 0:8] + cc[1:5, 0:8] * (w[0:4] + w[2:6] + beside_in_plane(next_own)[:, 0:8])
+        own, ring = disp[i], ring_w[i]
+        f, cc, c_r, c_f, c_x = f_own[i], c_own[...], ring_c[...], face_c[...], corner_c[...]
+        face, corner = face_w[i], corner_w[i]
+
+        def beside(w, ends):
+            wide = jnp.concatenate([ends[0:1], w, ends[1:2]], axis=0)
+            return wide[0:4] + wide[2:6]
+
+        def ends_of(w):
+            return jnp.concatenate([w[0:1], w[3:4]], axis=0)
+
+        zero = jnp.zeros((2, 8, 128), F32)
+        from_faces = jnp.concatenate([face[0:1], zero, face[1:2]], axis=0)
+        from_corners = jnp.concatenate([corner[0:1], zero, corner[1:2]], axis=0)
+        own_1 = alone[i] + cc * (from_faces + from_ring(ring))
+        ring_1 = ring_once[i] + c_r * (to_ring(own) + from_corners)
+        face_1 = face_once[i] + c_f * (ends_of(own) + from_ring(corner))
+        corner_1 = corner_once[i] + c_x * (ends_of(ring) + to_ring(face))
+        own_2 = keep * own_1 + f + cc * (beside(own_1, face_1) + sides(own_1, ring_1) + along_z(own_1))
+        ring_2 = ring_twice[i] + keep * ring_1 + c_r * (to_ring(own_1) + beside(ring_1, corner_1) + along_z(ring_1))
+        face_2 = face_twice[i] + keep * face_1 + c_f * (ends_of(own_1) + sides(face_1, corner_1) + along_z(face_1))
+        field[i] = keep * own_2 + f + cc * (beside(own_2, face_2) + sides(own_2, ring_2) + along_z(own_2))
         return carry
 
     lax.fori_loop(0, COMP, sweeps, 0, unroll=12)
@@ -287,21 +334,14 @@
     for peer in hi_peers:
         remote(ra.at[hi], ra.at[hi], ph_ss.at[0], ph_rs.at[0], peer).start()
 
-    to_row, from_row = iota((64, 64), 0), iota((64, 64), 1)
-    wanted = lax.rem(to_row, 16) // 2 * 8 + lax.rem(to_row, 2) * 4 + to_row // 16
-    reorder = onehot(from_row == wanted)
-
     def wait_all(region, at, peer):
         remote(region, region, ph_ss.at[at], ph_rs.at[at], peer).wait_recv()
 
     wait_all(ra.at[pl.ds(0, NHI - 1)], 0, hi_peers[0])
-    mine = dot(reorder, ra[...].reshape(64, 128).astype(BF16)).astype(BF16).reshape(4, 16, 128)
-    g[c, y] = mine
+    for k in range(4):
+        g[c, y, k] = jnp.concatenate([ra[:, k], ra[:, 4 + k]], axis=0).astype(BF16)
     for peer in y_peers:
         remote(g.at[c, y], g.at[c, y], ph_ss.at[1], ph_rs.at[1], peer).start()
-    wait_all(g.at[c, pl.ds(0, NY - 1)], 1, y_peers[0])
-    remote(g.at[c], g.at[c], ph_ss.at[2], ph_rs.at[2], core_peer).start()
-
     row_f = iota((COMP, 8, 128), 1)
     fvol_s[0] = pairs(field[:, 3])
     fvol_s[1] = pairs(field[:, 0])
@@ -309,8 +349,7 @@
         acc = jnp.zeros((COMP, 8, 128), F32)
         for p in range(4):
             shift = p + 1 if t == 0 else p
-            rolled = field[:, p] if shift == 0 else pltpu.roll(field[:, p], shift, 1)
-            acc = jnp.where(row_f == p, rolled, acc)
+            acc = jnp.where(row_f == p, rolled(field[:, p], shift, 1), acc)
         frep_s[t] = pairs(acc)
     fmoves = []
     for s in (0, 1):
@@ -325,6 +364,9 @@
         def _():
             dst[...] = jnp.zeros(dst.shape, BF16)
 
+
+    wait_all(g.at[c, pl.ds(0, NY - 1)], 1, y_peers[0])
+    remote(g.at[c], g.at[c], ph_ss.at[2], ph_rs.at[2], core_peer).start()
 
     wait_all(g.at[c], 2, core_peer)
 
@@ -378,7 +420,7 @@
         lane_f = iota((COMP, 8, 128), 2)
         total = total + jnp.where(lane_f == 0, 0.0, pltpu.roll(w, 1, 2))
         total = total + jnp.where(lane_f == 127, 0.0, pltpu.roll(w, 127, 2))
-        base[:, p] = keep * w + f_ext[:, p, 0:8] + c_ext[1 + p, 0:8][None] * total
+        base[:, p] = keep * w + f_own[:, p] + c_own[p][None] * total
 
     wait_all(wr.at[pl.ds(0, NXY - 1)], 4, core_peer)
 
@@ -442,12 +484,14 @@
             V((TILES, RANK, 256), BF16), V((TILES, RANK, 256), BF16),
             V((1, TILES), I32), V((1, TILES), I32), V((1, TILES), I32),
             V((2, 19, 16, 128), BF16), V((2, 19, 16, 128), BF16),
-            V((2, 26, 16, 128), BF16), V((2, 26, 16, 128), BF16),
+            V((2, 10, 16, 128), BF16), V((2, 10, 16, 128), BF16),
             V((2, 2, 4, 16, 128), BF16), V((2, 2, 4, 16, 128), BF16),
             V((2, 6, 16, 128), BF16), V((2, 6, 16, 128), BF16),
             V((2, 6, 16, 128), BF16), V((2, 6, 16, 128), BF16),
-            V((COMP, 6, 16, 128), F32), V((COMP, 4, 16, 128), F32), V((6, 16, 128), F32),
-            V((COMP, 2, 16, 128), F32), V((COMP, 2, 8, 128), F32),
+            V((COMP, 4, 8, 128), F32), V((COMP, 4, 8, 128), F32), V((4, 8, 128), F32),
+            V((COMP, 4, 8, 128), F32), V((COMP, 4, 8, 128), F32), V((COMP, 4, 8, 128), F32), V((4, 8, 128), F32),
+            V((COMP, 2, 8, 128), F32), V((COMP, 2, 8, 128), F32), V((COMP, 2, 8, 128), F32), V((2, 8, 128), F32),
+            V((COMP, 2, 8, 128), F32), V((COMP, 2, 8, 128), F32), V((2, 8, 128), F32),
             V((COMP, 4, 8, 128), F32), V((COMP, 4, 8, 128), F32), V((4, 8, 128), F32),
             V((256, TQ), BF16), V((TQ, 256), BF16), V((256, SLOTS), BF16), V((32, SLOTS), F32),
             V((8, SLOTS), F32), V((128, SLOTS), BF16), V((TILES, 128), BF16), V((TILES, TQ), F32),

time: 50.2 us -> 48.7 us (0.970)
  Pallas kernels: 49.4 us -> 47.9 us
    pallas_call x1, Pallas kernels: 47.8 us -> 46.3 us  [shards(): pl.pallas_call(body, out_shape=(jax.ShapeDtypeStruct((COMP, 4, 8, 128), F...]
where the time goes in v4:
time: 48.7 us; the launch traced here: 48.6 us
  Pallas kernels  47.9 us (98%)
  between operations  0.64 us (1%)
    pallas_call x1, Pallas kernels, shards(): pl.pallas_call(body, out_shape=(jax.ShapeDtypeStruct((COMP, 4, 8, 128), F...  46.3 us
    pallas_call x1, Pallas kernels, shards(): pl.pallas_call(hand_out, out_shape=(jax.ShapeDtypeStruct((COMP, 4, 8, 128...  1.63 us

profile of v4, /device:TPU:1, one launch (start us, length us, event | category | flops | bytes accessed | tf_op | source)
XLA Modules:
  0.0 48.6 jit_solution(8736169234413533128)
XLA Ops:
  0.6 46.3 %shard_map.130 = (f32[12,4,8,128]{3,2,1,0:T(8,128)}, f32[4,256]{1,0:T(4,128)}, f32[4,128]{1,0:T(4,128)}) custom-call(f32[12,4,8,128]{3,2,1,0:T(8,128)} %bitcast.7, f32[12,4,8,128]{3,2,1,0:T(8,128)} %bitcast.8, f32[4,8,128]{2,1,0:T(8,128)} %stiff_h.1, s32[1,128]{1,0:T(1,128)} %wcell_h.1, f32[3,128]{1,0:T(4,128)} %wnorm_h.1, s32[1,128]{1,0:T(1,128)} %bitcast.9, ...), custom_call_target="tpu_custom_call" | custom-call | tf_op jit(solution)/shard_map/pallas_call | solution.py:472
  47.0 1.6 %shard_map.131 = (f32[12,4,8,128]{3,2,1,0:T(8,128)}, f32[4,256]{1,0:T(4,128)}, f32[4,128]{1,0:T(4,128)}) custom-call(f32[12,4,8,128]{3,2,1,0:T(8,128)} %get-tuple-element.9.u, f32[4,256]{1,0:T(4,128)} %get-tuple-element.10.p, f32[4,128]{1,0:T(4,128)} %get-tuple-element.11.w), custom_call_target="tpu_custom_call" | custom-call | tf_op jit(solution)/shard_map/pallas_call | solution.py:521

commit v5 on v4

--- a/solution.py
+++ b/solution.py
@@ -74,16 +74,25 @@
     def vol_of(x_, zh_, y_, c_):
         return ((x_ * NZH + zh_) * NY + y_) * NC + c_
 
-    hi_peers = [(lax.rem(hi + j, NHI) * NLO + lo, r) for j in range(1, NHI)]
-    y_peers = [(vol_of(x, zh, lax.rem(y + j, NY), c), r) for j in range(1, NY)]
+    ring_x, ring_y = (2, 1, NX - 1), (4, 3, NY - 3, 2, NY - 2, 1, NY - 1)
+    flip_peers = [(vol_of(lax.rem(x + j, NX), 1 - zh, y, c), r) for j in ring_x + (0,)]
+    x_peers = [(vol_of(lax.rem(x + j, NX), zh, y, c), r) for j in ring_x]
+    hi_peers = flip_peers + x_peers
+    y_peers = [(vol_of(x, zh, lax.rem(y + j, NY), c), r) for j in ring_y]
     core_peer = (vol_of(x, zh, y, 1 - c), r)
     here = x * NLO + lo
 
-    def plane_peer(j):
-        at = lax.rem(here + j, NXY)
-        return at, (at // NLO * (NZH * NLO) + zh * NLO + lax.rem(at, NLO), r)
-
-    z_at = [(zh, lax.rem(r + j, NR)) for j in range(1, NR)] + [(1 - zh, lax.rem(r + j, NR)) for j in range(NR)]
+    hops = {}
+    for dx in range(NX):
+        for dy in range(NY):
+            for dc in range(NC):
+                hops[dx, dy, dc] = 2 * (min(dx, NX - dx) + min(dy, NY - dy)) + dc
+    plane_order = sorted(hops, key=lambda step: -hops[step])[:-1]
+    at_x = [lax.rem(x + d, NX) for d in range(NX)]
+    at_y = [lax.rem(y + d, NY) for d in range(NY)]
+    at_c = [c, 1 - c]
+
+    z_at = [(1 - zh, lax.rem(r + j, NR)) for j in (0, 1, 3)] + [(zh, lax.rem(r + j, NR)) for j in (3, 1, 2)] + [(1 - zh, lax.rem(r + 2, NR))]
     z_peers = [(vol_of(x, zh_, y, c), r_) for zh_, r_ in z_at]
     up_v, down_v = lax.rem(v + 1, NV), lax.rem(v + NV - 1, NV)
     up_r, down_r = lax.rem(r + 1, NR), lax.rem(r + NR - 1, NR)
@@ -391,12 +400,9 @@
     back = jnp.concatenate([sums.reshape(16, 128), jnp.zeros((112, 128), F32)], axis=0).astype(BF16)
     ws[...] = dot_nt(sel_at[...], back).reshape(NXY, 1, 128)
 
-    def give_back(j, carry):
-        at, peer = plane_peer(j)
-        remote(ws.at[at], wr.at[here], ph_ss.at[4], ph_rs.at[4], peer).start()
-        return carry
-
-    lax.fori_loop(1, NXY, give_back, 0)
+    for dx, dy, dc in plane_order:
+        at = at_x[dx] * NLO + at_y[dy] * NC + at_c[dc]
+        remote(ws.at[at], wr.at[here], ph_ss.at[4], ph_rs.at[4], (vol_of(at_x[dx], zh, at_y[dy], at_c[dc]), r)).start()
     wr[here] = ws[here]
     own = jnp.where(zh == 0, sums[0], sums[1])
     wide = jnp.concatenate([own[0:4], own[4:8]], axis=1)

time: 48.7 us -> 47.5 us (0.975)
  Pallas kernels: 47.9 us -> 46.7 us
    pallas_call x1, Pallas kernels: 46.3 us -> 45.1 us  [shards(): pl.pallas_call(body, out_shape=(jax.ShapeDtypeStruct((COMP, 4, 8, 128), F...]
where the time goes in v5:
time: 47.5 us; the launch traced here: 47.4 us
  Pallas kernels  46.7 us (98%)
  between operations  0.64 us (1%)
    pallas_call x1, Pallas kernels, shards(): pl.pallas_call(body, out_shape=(jax.ShapeDtypeStruct((COMP, 4, 8, 128), F...  45.1 us
    pallas_call x1, Pallas kernels, shards(): pl.pallas_call(hand_out, out_shape=(jax.ShapeDtypeStruct((COMP, 4, 8, 128...  1.63 us

profile of v5, /device:TPU:1, one launch (start us, length us, event | category | flops | bytes accessed | tf_op | source)
XLA Modules:
  0.0 47.4 jit_solution(4370325692782654103)
XLA Ops:
  0.6 45.1 %shard_map.130 = (f32[12,4,8,128]{3,2,1,0:T(8,128)}, f32[4,256]{1,0:T(4,128)}, f32[4,128]{1,0:T(4,128)}) custom-call(f32[12,4,8,128]{3,2,1,0:T(8,128)} %bitcast.7, f32[12,4,8,128]{3,2,1,0:T(8,128)} %bitcast.8, f32[4,8,128]{2,1,0:T(8,128)} %stiff_h.1, s32[1,128]{1,0:T(1,128)} %wcell_h.1, f32[3,128]{1,0:T(4,128)} %wnorm_h.1, s32[1,128]{1,0:T(1,128)} %bitcast.9, ...), custom_call_target="tpu_custom_call" | custom-call | tf_op jit(solution)/shard_map/pallas_call | solution.py:478
  45.7 1.6 %shard_map.131 = (f32[12,4,8,128]{3,2,1,0:T(8,128)}, f32[4,256]{1,0:T(4,128)}, f32[4,128]{1,0:T(4,128)}) custom-call(f32[12,4,8,128]{3,2,1,0:T(8,128)} %get-tuple-element.9.u, f32[4,256]{1,0:T(4,128)} %get-tuple-element.10.p, f32[4,128]{1,0:T(4,128)} %get-tuple-element.11.w), custom_call_target="tpu_custom_call" | custom-call | tf_op jit(solution)/shard_map/pallas_call | solution.py:527

commit v6 on v5

--- a/solution.py
+++ b/solution.py
@@ -510,19 +510,24 @@
             pltpu.SemaphoreType.DMA((4,)), pltpu.SemaphoreType.DMA((4,)),
             pltpu.SemaphoreType.DMA((5,)), pltpu.SemaphoreType.DMA((5,)),
         ],
-        compiler_params=pltpu.CompilerParams(collective_id=0, has_side_effects=True, vmem_limit_bytes=56 << 20),
+        compiler_params=pltpu.CompilerParams(collective_id=0, has_side_effects=True, vmem_limit_bytes=40 << 20),
     )(
-        displacement.reshape(COMP, 4, 8, 128),
-        body_force.reshape(COMP, 4, 8, 128),
-        stiffness,
-        wet_cell,
-        wet_normal,
-        route.reshape(1, SLOTS),
-        tile_u,
-        tile_v,
-        tile_row.reshape(1, TILES),
-        tile_col.reshape(1, TILES),
-        tile_rank.reshape(1, TILES),
+        *(
+            pltpu.with_memory_space_constraint(array, pltpu.HBM)
+            for array in (
+                displacement.reshape(COMP, 4, 8, 128),
+                body_force.reshape(COMP, 4, 8, 128),
+                stiffness,
+                wet_cell,
+                wet_normal,
+                route.reshape(1, SLOTS),
+                tile_u,
+                tile_v,
+                tile_row.reshape(1, TILES),
+                tile_col.reshape(1, TILES),
+                tile_rank.reshape(1, TILES),
+            )
+        )
     )
     updated, pressure, wet = pl.pallas_call(
         hand_out,
@@ -533,7 +538,7 @@
         ),
         in_specs=[vmem] * 3,
         out_specs=(vmem, vmem, vmem),
-        compiler_params=pltpu.CompilerParams(vmem_limit_bytes=56 << 20),
+        compiler_params=pltpu.CompilerParams(vmem_limit_bytes=16 << 20),
     )(updated, pressure, wet)
     return updated.reshape(displacement.shape), pressure, wet
 

time: 47.5 us -> 45.9 us (0.966)
  Pallas kernels: 46.7 us -> 45.1 us
    pallas_call x1, Pallas kernels: 1.63 us -> 0.7 us  [shards(): pl.pallas_call(hand_out, out_shape=(jax.ShapeDtypeStruct((COMP, 4, 8, 128...]
    pallas_call x1, Pallas kernels: 45.1 us -> 44.4 us  [shards(): pl.pallas_call(body, out_shape=(jax.ShapeDtypeStruct((COMP, 4, 8, 128), F...]
where the time goes in v6:
time: 45.9 us; the launch traced here: 45.8 us
  Pallas kernels  45.1 us (98%)
  between operations  0.64 us (1%)
    pallas_call x1, Pallas kernels, shards(): pl.pallas_call(body, out_shape=(jax.ShapeDtypeStruct((COMP, 4, 8, 128), F...  44.4 us

profile of v6, /device:TPU:1, one launch (start us, length us, event | category | flops | bytes accessed | tf_op | source)
XLA Modules:
  0.0 45.8 jit_solution(15975171182891521337)
XLA Ops:
  0.6 44.4 %shard_map.130 = (f32[12,4,8,128]{3,2,1,0:T(8,128)S(1)}, f32[4,256]{1,0:T(4,128)S(1)}, f32[4,128]{1,0:T(4,128)S(1)}) custom-call(f32[12,4,8,128]{3,2,1,0:T(8,128)} %bitcast.7, f32[12,4,8,128]{3,2,1,0:T(8,128)} %bitcast.8, f32[4,8,128]{2,1,0:T(8,128)} %stiff_h.1, s32[1,128]{1,0:T(1,128)} %wcell_h.1, f32[3,128]{1,0:T(4,128)} %wnorm_h.1, s32[1,128]{1,0:T(1,128)} %bitcast.9, ...), custom_call_target="tpu_custom_call" | custom-call | tf_op jit(solution)/shard_map/pallas_call | solution.py:478
  45.1 0.7 %shard_map.131 = (f32[12,4,8,128]{3,2,1,0:T(8,128)}, f32[4,256]{1,0:T(4,128)}, f32[4,128]{1,0:T(4,128)}) custom-call(f32[12,4,8,128]{3,2,1,0:T(8,128)S(1)} %get-tuple-element.9.u, f32[4,256]{1,0:T(4,128)S(1)} %get-tuple-element.10.p, f32[4,128]{1,0:T(4,128)S(1)} %get-tuple-element.11.w), custom_call_target="tpu_custom_call" | custom-call | tf_op jit(solution)/shard_map/pallas_call | solution.py:532

commit v7 on v6

--- a/solution.py
+++ b/solution.py
@@ -257,7 +257,7 @@
     sel_t[...] = jnp.transpose(col_t)[0:TILES].astype(BF16)
 
     at_b, at_g = iota((256, 256), 0), iota((256, 256), 1)
-    source = lax.rem(at_b, 8) * 32 + lax.rem(at_b // 16, 8) * 4 + at_b // 128 * 2 + lax.rem(at_b // 8, 2)
+    source = lax.rem(at_b, 4) * 64 + lax.rem(at_b // 64, 2) * 32 + lax.rem(at_b // 8, 8) * 4 + at_b // 128 * 2 + lax.rem(at_b // 4, 2)
     perm_v = onehot(at_g == source)
     vdt[...] = dot_nt(perm_v, tv[...].reshape(TQ, 256)).astype(BF16)
     split = at_b == lax.rem(at_g, 128) * 2 + at_g // 128
@@ -339,18 +339,53 @@
     traces = jnp.concatenate([traces, traces], axis=0) * armask[...]
     message = dot_nt(traces.astype(BF16), place[...])
 
-    ra[hi] = message
-    for peer in hi_peers:
-        remote(ra.at[hi], ra.at[hi], ph_ss.at[0], ph_rs.at[0], peer).start()
+    ra[zh, x] = message
+    for peer in flip_peers:
+        remote(ra.at[zh, x], ra.at[zh, x], ph_ss.at[0], ph_rs.at[0], peer).start()
+    for peer in x_peers:
+        remote(ra.at[zh, x], ra.at[zh, x], ph_ss.at[5], ph_rs.at[5], peer).start()
 
     def wait_all(region, at, peer):
         remote(region, region, ph_ss.at[at], ph_rs.at[at], peer).wait_recv()
 
-    wait_all(ra.at[pl.ds(0, NHI - 1)], 0, hi_peers[0])
-    for k in range(4):
-        g[c, y, k] = jnp.concatenate([ra[:, k], ra[:, 4 + k]], axis=0).astype(BF16)
-    for peer in y_peers:
-        remote(g.at[c, y], g.at[c, y], ph_ss.at[1], ph_rs.at[1], peer).start()
+    def gather_y(z, at):
+        rows = []
+        for k in range(4):
+            rows += [ra[z, :, k], ra[z, :, 4 + k]]
+        g[c, z, y] = jnp.concatenate(rows, axis=0).astype(BF16).reshape(2, 16, 128)
+        for peer in y_peers:
+            remote(g.at[c, z, y], g.at[c, z, y], ph_ss.at[at], ph_rs.at[at], peer).start()
+
+    wait_all(ra.at[zh, pl.ds(0, NX - 1)], 5, core_peer)
+    gather_y(zh, 1)
+    wait_all(ra.at[1 - zh], 0, core_peer)
+    gather_y(1 - zh, 6)
+
+    wait_all(g.at[c, zh, pl.ds(0, NY - 1)], 1, core_peer)
+    remote(g.at[c, zh], g.at[c, zh], ph_ss.at[2], ph_rs.at[2], core_peer).start()
+    wait_all(g.at[c, 1 - zh, pl.ds(0, NY - 1)], 6, core_peer)
+    remote(g.at[c, 1 - zh], g.at[c, 1 - zh], ph_ss.at[7], ph_rs.at[7], core_peer).start()
+
+    wait_all(g.at[c, zh], 2, core_peer)
+    wait_all(g.at[c, 1 - zh], 7, core_peer)
+
+    pick = sel_t[...]
+    waves = g[...].astype(F32).reshape(NC, NZH, NY, 4, 8, 128)
+    waves = [waves[:, :, :, k].reshape(256, 128).astype(BF16) for k in range(4)]
+    chosen = jnp.concatenate([dot_nt(pick, wave) for wave in waves], axis=0).astype(BF16)
+    every = dot(chosen, vdt[...])
+    coef = jnp.sum(every.reshape(4, TILES, TQ) * diag_m[...][None], axis=1)
+    coef = jnp.concatenate([coef, coef], axis=0)
+    spread_c = (jnp.concatenate([coef] * 4, axis=0) * row_m[...]).astype(BF16)
+    parts = dot(spread_c, ud[...])
+    take = lax.rem(iota((32, 128), 0), 8) < 4
+    parts = jnp.where(take, parts[:, 0:128], parts[:, 128:256])
+    zs[...] = parts.reshape(4, 8, 128)
+
+    mine_at = zh * NR + r
+    for (zh_, r_), peer in zip(z_at, z_peers):
+        remote(zs.at[r_], zr.at[mine_at], ph_ss.at[3], ph_rs.at[3], peer).start()
+    zr[mine_at] = zs[r]
     row_f = iota((COMP, 8, 128), 1)
     fvol_s[0] = pairs(field[:, 3])
     fvol_s[1] = pairs(field[:, 0])
@@ -374,27 +409,6 @@
             dst[...] = jnp.zeros(dst.shape, BF16)
 
 
-    wait_all(g.at[c, pl.ds(0, NY - 1)], 1, y_peers[0])
-    remote(g.at[c], g.at[c], ph_ss.at[2], ph_rs.at[2], core_peer).start()
-
-    wait_all(g.at[c], 2, core_peer)
-
-    pick = sel_t[...]
-    chosen = jnp.concatenate([dot_nt(pick, g[:, :, k].reshape(256, 128)) for k in range(4)], axis=0).astype(BF16)
-    every = dot(chosen, vdt[...])
-    coef = jnp.sum(every.reshape(4, TILES, TQ) * diag_m[...][None], axis=1)
-    coef = jnp.concatenate([coef, coef], axis=0)
-    spread_c = (jnp.concatenate([coef] * 4, axis=0) * row_m[...]).astype(BF16)
-    parts = dot(spread_c, ud[...])
-    take = lax.rem(iota((32, 128), 0), 8) < 4
-    parts = jnp.where(take, parts[:, 0:128], parts[:, 128:256])
-    zs[...] = parts.reshape(4, 8, 128)
-
-    mine_at = zh * NR + r
-    for (zh_, r_), peer in zip(z_at, z_peers):
-        remote(zs.at[r_], zr.at[mine_at], ph_ss.at[3], ph_rs.at[3], peer).start()
-    zr[mine_at] = zs[r]
-
     wait_all(zr.at[pl.ds(0, 2 * NR - 1)], 3, z_peers[0])
     sums = jnp.sum(zr[...].reshape(NZH, NR, 8, 128), axis=1)
     back = jnp.concatenate([sums.reshape(16, 128), jnp.zeros((112, 128), F32)], axis=0).astype(BF16)
@@ -458,9 +472,12 @@
     def sent(region, at, peer):
         remote(region, region, ph_ss.at[at], ph_rs.at[at], peer).wait_send()
 
-    sent(ra.at[pl.ds(0, NHI - 1)], 0, hi_peers[0])
-    sent(g.at[c, pl.ds(0, NY - 1)], 1, y_peers[0])
-    sent(g.at[c], 2, core_peer)
+    sent(ra.at[1 - zh], 0, core_peer)
+    sent(ra.at[zh, pl.ds(0, NX - 1)], 5, core_peer)
+    for z, at in ((zh, 1), (1 - zh, 6)):
+        sent(g.at[c, z, pl.ds(0, NY - 1)], at, core_peer)
+    sent(g.at[c, zh], 2, core_peer)
+    sent(g.at[c, 1 - zh], 7, core_peer)
     sent(zr.at[pl.ds(0, 2 * NR - 1)], 3, z_peers[0])
     sent(wr.at[pl.ds(0, NXY - 1)], 4, core_peer)
 
@@ -502,13 +519,13 @@
             V((256, TQ), BF16), V((TQ, 256), BF16), V((256, SLOTS), BF16), V((32, SLOTS), F32),
             V((8, SLOTS), F32), V((128, SLOTS), BF16), V((TILES, 128), BF16), V((TILES, TQ), F32),
             V((32, TQ), F32), V((NXY, NV), BF16), V((SLOTS, 128), BF16), V((SLOTS, 128), F32),
-            V((NHI, 8, 128), F32), V((NC, NY, 4, 16, 128), BF16),
+            V((NZH, NX, 8, 128), F32), V((NC, NZH, NY, 2, 16, 128), BF16),
             V((NR, 8, 128), F32), V((NZH * NR, 8, 128), F32),
             V((NXY, 1, 128), F32), V((NXY, 1, 128), F32),
             pltpu.SemaphoreType.DMA((11,)),
             pltpu.SemaphoreType.DMA((8,)), pltpu.SemaphoreType.DMA((8,)),
             pltpu.SemaphoreType.DMA((4,)), pltpu.SemaphoreType.DMA((4,)),
-            pltpu.SemaphoreType.DMA((5,)), pltpu.SemaphoreType.DMA((5,)),
+            pltpu.SemaphoreType.DMA((8,)), pltpu.SemaphoreType.DMA((8,)),
         ],
         compiler_params=pltpu.CompilerParams(collective_id=0, has_side_effects=True, vmem_limit_bytes=40 << 20),
     )(

time: 45.9 us -> 45.8 us (level)
  no operation moved by 1% of the time
where the time goes in v7:
time: 45.8 us; the launch traced here: 45.7 us
  Pallas kernels  45 us (98%)
  between operations  0.64 us (1%)
    pallas_call x1, Pallas kernels, shards(): pl.pallas_call(body, out_shape=(jax.ShapeDtypeStruct((COMP, 4, 8, 128), F...  44.3 us

profile of v7, /device:TPU:1, one launch (start us, length us, event | category | flops | bytes accessed | tf_op | source)
XLA Modules:
  0.0 45.7 jit_solution(16700247813725747122)
XLA Ops:
  0.6 44.3 %shard_map.130 = (f32[12,4,8,128]{3,2,1,0:T(8,128)S(1)}, f32[4,256]{1,0:T(4,128)S(1)}, f32[4,128]{1,0:T(4,128)S(1)}) custom-call(f32[12,4,8,128]{3,2,1,0:T(8,128)} %bitcast.7, f32[12,4,8,128]{3,2,1,0:T(8,128)} %bitcast.8, f32[4,8,128]{2,1,0:T(8,128)} %stiff_h.1, s32[1,128]{1,0:T(1,128)} %wcell_h.1, f32[3,128]{1,0:T(4,128)} %wnorm_h.1, s32[1,128]{1,0:T(1,128)} %bitcast.9, ...), custom_call_target="tpu_custom_call" | custom-call | tf_op jit(solution)/shard_map/pallas_call | solution.py:495
  45.0 0.7 %shard_map.131 = (f32[12,4,8,128]{3,2,1,0:T(8,128)}, f32[4,256]{1,0:T(4,128)}, f32[4,128]{1,0:T(4,128)}) custom-call(f32[12,4,8,128]{3,2,1,0:T(8,128)S(1)} %get-tuple-element.9.u, f32[4,256]{1,0:T(4,128)S(1)} %get-tuple-element.10.p, f32[4,128]{1,0:T(4,128)S(1)} %get-tuple-element.11.w), custom_call_target="tpu_custom_call" | custom-call | tf_op jit(solution)/shard_map/pallas_call | solution.py:549

commit v8 on v6

--- a/solution.py
+++ b/solution.py
@@ -215,7 +215,7 @@
 
     pl.semaphore_wait(barrier, len(greeted))
 
-    for src, dst, at, dev, sends, comes in moves:
+    for src, dst, at, dev, sends, comes in moves[:6]:
         @pl.when(sends)
         def _():
             remote(src, dst, halo_ss.at[at], halo_rs.at[at], dev).start()
@@ -244,6 +244,11 @@
     za_hot[...] = jnp.transpose(za_t)
     at_row = iota((NXY, NV), 0)
     sel_at[...] = onehot(iota((NXY, NV), 1) == at_row // NLO * (NZH * NLO) + zh * NLO + lax.rem(at_row, NLO))
+
+    for src, dst, at, dev, sends, comes in moves[6:]:
+        @pl.when(sends)
+        def _():
+            remote(src, dst, halo_ss.at[at], halo_rs.at[at], dev).start()
 
     spread = onehot(iota((TILES, TQ), 1) // RANK == iota((TILES, TQ), 0))
     lists = jnp.concatenate([jnp.broadcast_to(trank[...], (4, TILES)), jnp.broadcast_to(trow[...], (4, TILES))], axis=0)

time: 45.9 us -> 45.9 us (level)
  no operation moved by 1% of the time
where the time goes in v8:
time: 45.9 us; the launch traced here: 45.8 us
  Pallas kernels  45.1 us (98%)
  between operations  0.64 us (1%)
    pallas_call x1, Pallas kernels, shards(): pl.pallas_call(body, out_shape=(jax.ShapeDtypeStruct((COMP, 4, 8, 128), F...  44.4 us

profile of v8, /device:TPU:1, one launch (start us, length us, event | category | flops | bytes accessed | tf_op | source)
XLA Modules:
  0.0 45.8 jit_solution(10570861622674856695)
XLA Ops:
  0.6 44.4 %shard_map.130 = (f32[12,4,8,128]{3,2,1,0:T(8,128)S(1)}, f32[4,256]{1,0:T(4,128)S(1)}, f32[4,128]{1,0:T(4,128)S(1)}) custom-call(f32[12,4,8,128]{3,2,1,0:T(8,128)} %bitcast.7, f32[12,4,8,128]{3,2,1,0:T(8,128)} %bitcast.8, f32[4,8,128]{2,1,0:T(8,128)} %stiff_h.1, s32[1,128]{1,0:T(1,128)} %wcell_h.1, f32[3,128]{1,0:T(4,128)} %wnorm_h.1, s32[1,128]{1,0:T(1,128)} %bitcast.9, ...), custom_call_target="tpu_custom_call" | custom-call | tf_op jit(solution)/shard_map/pallas_call | solution.py:483
  45.1 0.7 %shard_map.131 = (f32[12,4,8,128]{3,2,1,0:T(8,128)}, f32[4,256]{1,0:T(4,128)}, f32[4,128]{1,0:T(4,128)}) custom-call(f32[12,4,8,128]{3,2,1,0:T(8,128)S(1)} %get-tuple-element.9.u, f32[4,256]{1,0:T(4,128)S(1)} %get-tuple-element.10.p, f32[4,128]{1,0:T(4,128)S(1)} %get-tuple-element.11.w), custom_call_target="tpu_custom_call" | custom-call | tf_op jit(solution)/shard_map/pallas_call | solution.py:537
